TPU v7x, 512 devices: a whole 4x8x8 slice. The times are simulated.
512 devices in a mesh: dp: 16 (over x, y_hi), slab: 32 (over z, y_lo, core).
Axes of the slice: x: 4, y: 8 (y_hi: 4, y_lo: 2; y = y_hi * 2 + y_lo), z: 8, core: 2. Of those that a mesh axis runs over, the one named last changes fastest.
Arguments:
- sensitivity: bfloat16 [12288, 98304], P('dp', 'slab'), may hold values from -6 to 6
- panel_index: int32 [1], replicated, may hold values from 0 to 47
- cell_class: int32 [96, 1024], P('slab'), may hold values from 0 to 7
- tear_layer: int32 [1024], replicated, may hold values from 1 to 95
- coef_table: float32 [3, 2, 8], replicated, may hold values from 0.02 to 0.1
Outputs:
- panel_block: float32 [12288, 128], P(('dp', 'slab'))
All inputs are finite; a program needn't handle non-finite values.
Results may differ from a plain program's by a relative error of at most 0.0015.
Values may be sent and summed in bfloat16 or wider, within the bound.
A program may use at most 64 MiB of HBM per device.

v0:
```python
import math

import jax
import jax.numpy as jnp
from jax import lax
from jax.sharding import PartitionSpec as P

HY = 32
PANEL = 128
PANELS_DEV = 6


def padded_2(block, sides, width):
    for axis, dim in sides:
        count = lax.axis_size(axis)
        forward = [(i, i + 1) for i in range(count - 1)]
        backward = [(target, source) for source, target in forward]
        low = lax.ppermute(
            lax.slice_in_dim(block, block.shape[dim] - width, None, axis=dim), axis, forward
        )
        high = lax.ppermute(lax.slice_in_dim(block, 0, width, axis=dim), axis, backward)
        block = jnp.concatenate([low, block, high], axis=dim)
    return block


def spread(block, axis, owner):
    block = jnp.where(lax.axis_index(axis) == owner, block, jnp.zeros_like(block))
    return lax.psum(block, axis)


def horizontal(field, width_y):
    count = field.shape[-1]
    padded = jnp.pad(field, ((0, 0), (0, 0), (width_y, width_y)))
    north = padded[..., :count]
    south = padded[..., 2 * width_y :]
    column = jnp.arange(count) % width_y
    west = jnp.where(column > 0, padded[..., width_y - 1 : width_y - 1 + count], 0.0)
    east = jnp.where(column < width_y - 1, padded[..., width_y + 1 : width_y + 1 + count], 0.0)
    return north + south + west + east - 4.0 * field


def sweep(extended, classes, tear_layer, coef_table, number, first, layers, width_y):
    middle = extended[:, 1:-1]
    upper = extended[:, :-2]
    lower = extended[:, 2:]
    count = middle.shape[1]
    layer = first + 1 + jnp.arange(count, dtype=jnp.int32)
    open_up = (tear_layer[None, :] != layer[:, None]).astype(jnp.float32)
    open_down = (tear_layer[None, :] != (layer + 1)[:, None]).astype(jnp.float32)
    inner = classes[1:-1]
    coef_h = jnp.zeros(inner.shape, jnp.float32)
    coef_v = jnp.zeros(inner.shape, jnp.float32)
    for level in range(coef_table.shape[2]):
        coef_h = jnp.where(inner == level, coef_table[number, 0, level], coef_h)
        coef_v = jnp.where(inner == level, coef_table[number, 1, level], coef_v)
    vertical = open_up * (upper - middle) + open_down * (lower - middle)
    updated = middle + coef_h * horizontal(middle, width_y) + 4.0 * coef_v * vertical
    valid = ((layer >= 0) & (layer < layers)).astype(jnp.float32)[:, None]
    return updated * valid


def blockwise(action, extended):
    total_rows = extended.shape[0]
    block_rows = 32
    stacked = extended.reshape((total_rows // block_rows, block_rows) + extended.shape[1:])
    result = lax.map(action, stacked)
    return result.reshape((total_rows,) + result.shape[2:])


def smooth_field(field, cell_class, tear_layer, coef_table):
    depth = field.shape[1]
    layers = depth * lax.axis_size("slab")
    first_layer = lax.axis_index("slab") * depth
    sweeps_total = coef_table.shape[0]
    padded_class = jnp.pad(cell_class, ((1, 1), (0, 0)))
    for number in range(sweeps_total):
        extended = padded_2(field, (("slab", 1),), 1)

        def one_sweep(block, number=number):
            return sweep(
                block, padded_class, tear_layer, coef_table, number, first_layer - 1, layers, HY
            )

        field = blockwise(one_sweep, extended)
    return field


def body(sensitivity, panel_index, cell_class, tear_layer, coef_table):
    start = panel_index[0]
    data_rows = sensitivity.shape[0]
    cell_count = sensitivity.shape[1]
    plane = cell_class.shape[1]
    depth = cell_class.shape[0]
    owner = start // PANELS_DEV
    offset = start % PANELS_DEV * PANEL
    local_rows = lax.dynamic_slice_in_dim(sensitivity, offset, PANEL, 0)
    panel_rows = spread(local_rows, "dp", owner)
    field = panel_rows.astype(jnp.float32).reshape(PANEL, depth, plane)
    field = smooth_field(field, cell_class, tear_layer, coef_table)
    smoothed = field.reshape(PANEL, cell_count).astype(jnp.bfloat16)
    out_rows = data_rows // lax.axis_size("slab")
    summed = lax.psum_scatter(
        lax.dot_general(
            sensitivity, smoothed, (((1,), (1,)), ((), ())), preferred_element_type=jnp.float32
        ),
        "slab",
        scatter_dimension=0,
        tiled=True,
    )
    total_cells = depth * lax.axis_size("slab") * plane
    summed = summed * (1.0 / math.sqrt(total_cells))
    base = lax.axis_index("dp") * data_rows + lax.axis_index("slab") * out_rows
    row_index = base + jnp.arange(out_rows, dtype=jnp.int32)[:, None]
    col_index = jnp.arange(PANEL, dtype=jnp.int32)[None, :]
    keep = row_index >= start * PANEL + col_index
    return jnp.where(keep, summed, 0.0)


def solution(mesh):
    return jax.shard_map(
        body,
        mesh=mesh,
        in_specs=(P("dp", "slab"), P(), P("slab", None), P(), P()),
        out_specs=P(("dp", "slab"), None),
        check_vma=False,
    )
```

profile of v0, /device:TPU:1, one launch (start us, length us, event | category | flops | bytes accessed | tf_op | source)
XLA Modules:
  0.0 659.8 jit_solution(1360716585937653933)
XLA Ops:
  9.9 169.6 %all-reduce.8.cloned.1.call-done = bf16[128,3072]{0,1:T(8,128)(2,1)} async-done(((bf16[128,3072]{0,1:T(8,128)(2,1)}), bf16[128,3072]{0,1:T(8,128)(2,1)}) %all-reduce.8.cloned.1.call-update) | async-done | bytes 786448 | tf_op jit(solution)/shard_map/psum | solution.py:28
  179.5 1.3 convert_element_type.109
  181.7 13.1 %collective-permute-start = (f32[128,1,1024]{0,2,1:T(8,128)S(1)}, f32[128,1,1024]{0,2,1:T(8,128)S(1)}, u32[]{:S(2)}, u32[]{:S(2)}) collective-permute-start(f32[128,1,1024]{0,2,1:T(8,128)S(1)} %get-tuple-element.432), channel_id=1, source_target_pairs={{0,1},{1,2},{2,3},{3,4},{4,5},{5,6},{6,7},{7,8},{8,9},{9,10},{10,1... | collective-permute-start | bytes 1572872 | tf_op jit(solution)/shard_map/ppermute | solution.py:18
  194.8 1.9 collective-permute-start.1
  196.8 1.5 copy.21
  198.3 2.8 concatenate.27
  201.9 7.7 %collective-permute-done.1 = f32[128,1,1024]{0,2,1:T(8,128)} collective-permute-done((f32[128,1,1024]{0,2,1:T(8,128)}, f32[128,1,1024]{0,2,1:T(8,128)}, u32[]{:S(2)}, u32[]{:S(2)}) %collective-permute-start.1) | collective-permute-done | bytes 524320 | tf_op jit(solution)/shard_map/ppermute | solution.py:21
  209.6 2.1 copy.22
  211.7 1.6 copy.24
  213.3 3.3 pad_maximum_fusion
  217.2 55.5 %while.36 = (s32[]{:T(128)}, f32[4,32,3,1024]{3,2,1,0:T(4,128)S(1)}, f32[4,32,5,1024]{3,2,1,0:T(8,128)}, s32[5,1024]{1,0:T(8,128)S(1)}, f32[3,2,8]{2,1,0:T(2,128...) while((s32[]{:T(128)}, f32[4,32,3,1024]{3,2,1,0:T(4,128)S(1)}, f32[4,32,5,1024]{3,2,1,0:T(8,128)}, ...), condition=%wide.region_2.3_spmd, body=%wide.region_1.2_spmd.sunk | while | flops 1768471 | bytes 4379489 | solution.py:66
  217.9 5.1 select_select_fusion.6
  223.0 5.1 select_multiply_fusion.6
  228.1 1.3 dynamic-slice_bitcast_fusion.6
  229.6 1.4 fusion.62
  231.8 5.1 select_select_fusion.6
  236.8 5.1 select_multiply_fusion.6
  242.0 1.3 dynamic-slice_bitcast_fusion.6
  243.5 1.4 fusion.62
  245.7 5.1 select_select_fusion.6
  250.7 5.1 select_multiply_fusion.6
  255.9 1.3 dynamic-slice_bitcast_fusion.6
  257.4 1.4 fusion.62
  259.5 5.1 select_select_fusion.6
  264.6 5.1 select_multiply_fusion.6
  271.3 1.4 fusion.62
  272.7 1.8 fusion.47
  274.5 1.9 collective-permute-start.2
  276.4 2.6 collective-permute-start.3
  279.0 3.8 collective-permute-done.2
  282.8 7.8 %collective-permute-done.3 = f32[128,1,1024]{2,1,0:T(1,128)S(1)} collective-permute-done((f32[128,1,1024]{2,1,0:T(1,128)}, f32[128,1,1024]{2,1,0:T(1,128)S(1)}, u32[]{:S(2)}, u32[]{:S(2)}) %collective-permute-start.3) | collective-permute-done | bytes 524320 | tf_op jit(solution)/shard_map/ppermute | solution.py:21
  290.6 3.3 pad_maximum_fusion.1
  294.5 55.5 %while.37 = (s32[]{:T(128)}, f32[4,32,3,1024]{3,2,1,0:T(4,128)S(1)}, f32[4,32,5,1024]{3,2,1,0:T(8,128)}, s32[5,1024]{1,0:T(8,128)S(1)}, f32[3,2,8]{2,1,0:T(2,128...) while((s32[]{:T(128)}, f32[4,32,3,1024]{3,2,1,0:T(4,128)S(1)}, f32[4,32,5,1024]{3,2,1,0:T(8,128)}, ...), condition=%wide.region_4.5_spmd, body=%wide.region_3.4_spmd.sunk | while | flops 1768471 | bytes 4379489 | solution.py:66
  295.2 5.1 select_select_fusion.7
  300.3 5.1 select_multiply_fusion.7
  305.5 1.3 dynamic-slice_bitcast_fusion.7
  307.0 1.4 fusion.65
  309.1 5.1 select_select_fusion.7
  314.2 5.1 select_multiply_fusion.7
  319.4 1.3 dynamic-slice_bitcast_fusion.7
  320.9 1.4 fusion.65
  323.0 5.1 select_select_fusion.7
  328.1 5.1 select_multiply_fusion.7
  333.3 1.3 dynamic-slice_bitcast_fusion.7
  334.7 1.4 fusion.65
  336.9 5.1 select_select_fusion.7
  342.0 5.1 select_multiply_fusion.7
  348.6 1.4 fusion.65
  350.9 1.9 collective-permute-start.4
  352.8 2.4 collective-permute-start.5
  355.6 3.3 collective-permute-done.4
  358.9 6.8 %collective-permute-done.5 = f32[128,1,1024]{2,1,0:T(1,128)S(1)} collective-permute-done((f32[128,1,1024]{2,1,0:T(1,128)S(1)}, f32[128,1,1024]{2,1,0:T(1,128)S(1)}, u32[]{:S(2)}, u32[]{:S(2)}) %collective-permute-start.5) | collective-permute-done | bytes 524320 | tf_op jit(solution)/shard_map/ppermute | solution.py:21
  365.7 3.3 pad_maximum_fusion.2
  369.1 54.9 %while.38 = (s32[]{:T(128)}, bf16[4,32,3,1024]{3,2,1,0:T(4,128)(2,1)S(1)}, f32[4,32,5,1024]{3,2,1,0:T(8,128)}, s32[5,1024]{1,0:T(8,128)S(1)}, f32[3,2,8]{2,1,0:T...) while((s32[]{:T(128)}, bf16[4,32,3,1024]{3,2,1,0:T(4,128)(2,1)S(1)}, f32[4,32,5,1024]{3,2,1,0:T(8,128)}, ...), condition=%wide.region_6.7_spmd, body=%wide.region_5.6_spmd.sunk | while | flops 1768471 | bytes 4379489 | solution.py:66
  369.8 5.1 select_select_fusion.8
  374.8 5.1 select_multiply_fusion.8
  383.5 5.1 select_select_fusion.8
  388.6 5.1 select_multiply_fusion.8
  397.2 5.1 select_select_fusion.8
  402.3 5.1 select_multiply_fusion.8
  411.0 5.1 select_select_fusion.8
  416.0 5.1 select_multiply_fusion.8
  424.3 4.8 convolution_bitcast_fusion
  431.1 220.2 %all-reduce.10.cloned.1.call-done = f32[768,128]{0,1:T(8,128)} async-done(((f32[768,128]{0,1:T(8,128)}), f32[768,128]{0,1:T(8,128)}) %all-reduce.10.cloned.1.call-update) | async-done | bytes 393232
  (112 shorter events, 34.0 us)
Async XLA Ops:
  6.5 173.0 %all-reduce.8.cloned.1.call-start = ((), (), s32[]{:S(2)}) async-start(), calls=%async_computation | async-start | bytes 1572864 | tf_op jit(solution)/shard_map/psum | solution.py:28
  8.4 188.3 %copy-start.3 = (s32[3,1024]{1,0:T(4,128)S(1)}, s32[3,1024]{1,0:T(4,128)}, u32[]{:S(2)}) copy-start(s32[3,1024]{1,0:T(4,128)} %param.13) | copy-start | bytes 36868
  9.8 641.5 %all-reduce.10.cloned.1.call-start = ((), (), s32[]{:S(2)}) async-start(), calls=%async_computation.1 | async-start | bytes 786432
  179.5 17.3 %copy-start.1 = (bf16[128,3072]{0,1:T(8,128)(2,1)S(1)}, bf16[128,3072]{0,1:T(8,128)(2,1)}, u32[]{:S(2)}) copy-start(bf16[128,3072]{0,1:T(8,128)(2,1)} %all-reduce.8.cloned.1.call-done) | copy-start | bytes 2359300
  181.7 19.4 %collective-permute-start = (f32[128,1,1024]{0,2,1:T(8,128)S(1)}, f32[128,1,1024]{0,2,1:T(8,128)S(1)}, u32[]{:S(2)}, u32[]{:S(2)}) collective-permute-start(f32[128,1,1024]{0,2,1:T(8,128)S(1)} %get-tuple-element.432), channel_id=1, source_target_pairs={{0,1},{1,2},{2,3},{3,4},{4,5},{5,6},{6,7},{7,8},{8,9},{9,10},{10,1... | collective-permute-start | bytes 1572872 | tf_op jit(solution)/shard_map/ppermute | solution.py:18
  194.8 14.8 %collective-permute-start.1 = (f32[128,1,1024]{0,2,1:T(8,128)}, f32[128,1,1024]{0,2,1:T(8,128)}, u32[]{:S(2)}, u32[]{:S(2)}) collective-permute-start(f32[128,1,1024]{0,2,1:T(8,128)} %get-tuple-element.433), channel_id=1, source_target_pairs={{1,0},{2,1},{3,2},{4,3},{5,4},{6,5},{7,6},{8,7},{9,8},{10,9},{11,1... | collective-permute-start | bytes 1572872 | tf_op jit(solution)/shard_map/ppermute | solution.py:21
  213.2 3.9 copy-start
  213.3 3.9 copy-start.2
  274.5 8.3 %collective-permute-start.2 = (f32[128,1,1024]{2,1,0:T(1,128)}, f32[128,1,1024]{2,1,0:T(1,128)S(1)}, u32[]{:S(2)}, u32[]{:S(2)}) collective-permute-start(f32[128,1,1024]{2,1,0:T(1,128)} %get-tuple-element.430), channel_id=1, source_target_pairs={{0,1},{1,2},{2,3},{3,4},{4,5},{5,6},{6,7},{7,8},{8,9},{9,10},{10,1... | collective-permute-start | bytes 1572872 | tf_op jit(solution)/shard_map/ppermute | solution.py:18
  276.4 14.2 %collective-permute-start.3 = (f32[128,1,1024]{2,1,0:T(1,128)}, f32[128,1,1024]{2,1,0:T(1,128)S(1)}, u32[]{:S(2)}, u32[]{:S(2)}) collective-permute-start(f32[128,1,1024]{2,1,0:T(1,128)} %get-tuple-element.431), channel_id=1, source_target_pairs={{1,0},{2,1},{3,2},{4,3},{5,4},{6,5},{7,6},{8,7},{9,8},{10,9},{11,1... | collective-permute-start | bytes 1572872 | tf_op jit(solution)/shard_map/ppermute | solution.py:21
  350.9 8.0 %collective-permute-start.4 = (f32[128,1,1024]{2,1,0:T(1,128)S(1)}, f32[128,1,1024]{2,1,0:T(1,128)S(1)}, u32[]{:S(2)}, u32[]{:S(2)}) collective-permute-start(f32[128,1,1024]{2,1,0:T(1,128)S(1)} %get-tuple-element.428), channel_id=1, source_target_pairs={{0,1},{1,2},{2,3},{3,4},{4,5},{5,6},{6,7},{7,8},{8,9},{9,10},{10,1... | collective-permute-start | bytes 1572872 | tf_op jit(solution)/shard_map/ppermute | solution.py:18
  352.8 12.9 %collective-permute-start.5 = (f32[128,1,1024]{2,1,0:T(1,128)S(1)}, f32[128,1,1024]{2,1,0:T(1,128)S(1)}, u32[]{:S(2)}, u32[]{:S(2)}) collective-permute-start(f32[128,1,1024]{2,1,0:T(1,128)S(1)} %get-tuple-element.429), channel_id=1, source_target_pairs={{1,0},{2,1},{3,2},{4,3},{5,4},{6,5},{7,6},{8,7},{9,8},{10,9},{11,1... | collective-permute-start | bytes 1572872 | tf_op jit(solution)/shard_map/ppermute | solution.py:21
Sparse Core Ops, SparseCore 0:
  10.3 169.2 all-reduce.7
  429.3 222.0 all-reduce.9
where the time goes:
time: 663 us; the launch traced here: 660 us
  waiting for transfers between devices  419 us (63%)
  other arithmetic  153 us (23%)
  local copies, waits for them, and re-layouts  43 us (6%)
  starting transfers between devices  23.9 us (4%)
  between operations  15 us (2%)
    unnamed x3, waiting for transfers between devices  220 us
    psum x1, waiting for transfers between devices, spread(): return lax.psum(block, axis)  170 us
    mul x12, other arithmetic, sweep(): 4.0 * coef_v * vertical  61.1 us
    select_n x12, other arithmetic, sweep(): coef_h = jnp.where(inner == level, coef_table[number, 0, level], coef_h)  60.7 us
    ppermute x3, waiting for transfers between devices, padded_2(): lax.ppermute(lax.slice_in_dim(block, 0, width, axis=dim), axis, backward)  22.4 us
    ppermute x3, starting transfers between devices, padded_2(): lax.ppermute(lax.slice_in_dim(block, block.shape[dim] - width, None, axis...  16.9 us
    dynamic_update_slice x12, other arithmetic, blockwise(): result = lax.map(action, stacked)  16.4 us
    squeeze x12, local copies, waits for them, and re-layouts, blockwise(): result = lax.map(action, stacked)  15.5 us
  transfers between devices with their start and end apart: 8, of which 7 were waited for; matrix products, arithmetic and copies ran while one was open for 1% of the time, Pallas kernels for 0%

commit v1 on v0

v1 whole, which is shorter than its diff:
```python
import functools
import math

import jax
import jax.numpy as jnp
from jax import lax
from jax.experimental import pallas as pl
from jax.experimental.pallas import tpu as pltpu
from jax.sharding import PartitionSpec as P

WIDTH_Y = 32
PANEL = 128
GROUP = 32
PIECE = 8
CHUNK = 384
VMEM_LIMIT = 63 * 1024 * 1024


def kernel(
    slabs,
    panel_hbm,
    table_hbm,
    sens_hbm,
    class_hbm,
    tear_hbm,
    out_ref,
    panel_ref,
    table_ref,
    class_ref,
    tear_ref,
    sens,
    send1,
    recv_early,
    recv_late,
    fwd1,
    pair1,
    chosen1,
    send2,
    recv2,
    raw,
    halo,
    class_halo,
    class_ext,
    coef,
    field,
    gath,
    panel,
    product,
    sibling_in,
    part,
    parts_in,
    load_sem,
    class_send,
    class_recv,
    s1_send,
    s1_recv,
    s2_send,
    s2_recv,
    h_send,
    h_recv,
    g5_send,
    g5_recv,
    g6_send,
    g6_recv,
    sib_send,
    sib_recv,
    rs_send,
    rs_recv,
):
    f32 = jnp.float32
    bf16 = jnp.bfloat16
    dp = lax.axis_index("dp")
    me = lax.axis_index("slab")
    x = lax.div(dp, 4)
    yh = lax.rem(dp, 4)
    groups, _, cells = sens.shape
    chips = slabs // 2
    core = lax.rem(me, 2)
    chip = lax.div(me, 2)
    sibling = me + 1 - 2 * core
    depth, plane = class_ref.shape
    layers = depth * slabs
    out_rows = out_ref.shape[0]
    panels_dev = groups * GROUP // PANEL
    right = lax.rem(x + 1, 4)
    left = lax.rem(x + 3, 4)
    before = lax.rem(me + slabs - 1, slabs)
    after = lax.rem(me + 1, slabs)

    def at(x_to, y_to, slab_to):
        return (x_to * 4 + y_to, slab_to)

    def remote(src, dst, send_sem, recv_sem, target):
        return pltpu.make_async_remote_copy(
            src_ref=src,
            dst_ref=dst,
            send_sem=send_sem,
            recv_sem=recv_sem,
            device_id=target,
            device_id_type=pl.DeviceIdType.MESH,
        )

    loads = 4

    def load(i):
        part_of = pl.ds(i * (groups // loads), groups // loads)
        return pltpu.make_async_copy(sens_hbm.at[part_of], sens.at[part_of], load_sem.at[0])

    small = [
        pltpu.make_async_copy(source, target, load_sem.at[1 + i])
        for i, (source, target) in enumerate(
            [(class_hbm, class_ref), (tear_hbm, tear_ref), (table_hbm, table_ref), (panel_hbm, panel_ref)]
        )
    ]
    for copy in small:
        copy.start()
    for i in range(loads):
        load(i).start()

    barrier = pltpu.get_barrier_semaphore()

    def greet(target):
        pl.semaphore_signal(
            barrier, inc=1, device_id=target, device_id_type=pl.DeviceIdType.MESH
        )

    greet(at(right, yh, me))
    greet(at(left, yh, me))
    for dj in (1, 2, 3):
        greet(at(x, lax.rem(yh + dj, 4), me))

    greet((dp, before))
    greet((dp, after))

    @pl.loop(1, chips)
    def _(d):
        greet((dp, lax.rem(me + 2 * d, slabs)))

    for copy in small:
        copy.wait()
    pltpu.make_async_copy(sens_hbm, sens, load_sem.at[0]).wait()

    start = panel_ref[0]
    owner = lax.div(start, panels_dev)
    x_owner = lax.div(owner, 4)
    y_owner = lax.rem(owner, 4)
    first_group = lax.rem(start, panels_dev) * 4

    @pl.when(x < 2)
    def _():
        for q in range(4):
            rows = sens[first_group + q].astype(f32).reshape(4, PIECE, cells).astype(bf16)
            for j in range(4):
                send1[q, lax.rem(j - yh + 6, 4)] = rows[j]

    pl.semaphore_wait(barrier, 7 + chips - 1)

    class_after = remote(class_ref, class_halo.at[0], class_send.at[0], class_recv.at[0], (dp, after))
    class_before = remote(class_ref, class_halo.at[1], class_send.at[1], class_recv.at[1], (dp, before))
    class_after.start()
    class_before.start()

    def early(q):
        return send1.at[q, 0:2]

    def late(q):
        return send1.at[q, 2:4]

    mate = at(1 - x, yh, me)
    outer = at(3 - x, yh, me)
    copy_far = remote(early(x + 2), fwd1, s1_send.at[0], s1_recv.at[0], outer)
    copy_in = remote(early(1 - x), recv_early.at[x], s1_send.at[1], s1_recv.at[1], mate)
    copy_mate = remote(late(x + 2), pair1.at[x], s1_send.at[2], s1_recv.at[2], mate)
    copy_out = remote(early(3 - x), recv_early.at[x], s1_send.at[3], s1_recv.at[3], outer)
    copy_in_late = remote(late(1 - x), recv_late.at[x], s1_send.at[4], s1_recv.at[4], mate)
    copy_chosen = remote(chosen1, recv_late.at[0], s1_send.at[5], s1_recv.at[5], outer)
    copy_on = remote(fwd1, recv_early.at[3 - x], s1_send.at[1], s1_recv.at[1], at(5 - x, yh, me))

    def arrived(slot, to):
        remote(to, to, s1_send.at[slot], s1_recv.at[slot], at(right, yh, me)).wait_recv()

    @pl.when(x < 2)
    def _():
        for copy in (copy_far, copy_in, copy_mate, copy_out, copy_in_late):
            copy.start()
        recv_early[x] = send1[x, 0:2]
        recv_late[x] = send1[x, 2:4]
        pair1[x] = send1[3 - x, 2:4]

    class_after.wait_recv()
    class_before.wait_recv()
    class_ext[0:2] = class_halo[0, depth - 2 : depth]
    class_ext[2 : 2 + depth] = class_ref[...]
    class_ext[2 + depth : 4 + depth] = class_halo[1, 0:2]
    class_ext[4 + depth :] = jnp.zeros_like(class_ext[4 + depth :])
    classes = class_ext[...]
    layer = me * depth - 2 + lax.broadcasted_iota(jnp.int32, classes.shape, 0)
    valid = (layer >= 0) & (layer < layers)
    tear = jnp.broadcast_to(tear_ref[...], classes.shape)
    open_up = tear != layer
    open_down = tear != layer + 1
    for k in range(table_ref.shape[0]):
        a = jnp.zeros(classes.shape, f32)
        b = jnp.zeros(classes.shape, f32)
        for level in range(table_ref.shape[2]):
            a = jnp.where(classes == level, table_ref[k, 0, level], a)
            b = jnp.where(classes == level, table_ref[k, 1, level], b)
        a = jnp.where(valid, a, 0.0)
        b = jnp.where(valid, 4.0 * b, 0.0)
        up = jnp.where(open_up, b, 0.0)
        down = jnp.where(open_down, b, 0.0)
        coef[k, 0] = 1.0 - 4.0 * a - up - down
        coef[k, 1] = a
        coef[k, 2] = up
        coef[k, 3] = down

    def copy_y(dj):
        return remote(
            send2.at[dj], recv2.at[yh], s2_send.at[dj], s2_recv.at[yh], at(x, lax.rem(yh + dj, 4), me)
        )

    def wait_y(dj):
        j = lax.rem(yh + dj, 4)
        remote(send2.at[dj], recv2.at[j], s2_send.at[dj], s2_recv.at[j], at(x, j, me)).wait_recv()

    @pl.when(x >= 2)
    def _():
        arrived(0, fwd1)
        copy_on.start()
        arrived(3, recv_early.at[3 - x])

    arrived(1, recv_early.at[jnp.where(x < 2, 1 - x, x - 2)])
    chosen = recv_early[x_owner]
    send2[2] = chosen[0]
    copy_y(2).start()
    send2[3] = chosen[1]
    copy_y(3).start()

    @pl.when(x < 2)
    def _():
        arrived(2, pair1.at[1 - x])
        chosen1[...] = pair1[x_owner]
        copy_chosen.start()
        arrived(4, recv_late.at[1 - x])

    @pl.when(x >= 2)
    def _():
        arrived(5, recv_late.at[0])

    chosen = recv_late[jnp.where(x < 2, x_owner, 0)]
    send2[1] = chosen[1]
    copy_y(1).start()
    recv2[yh] = chosen[0]
    for dj in (2, 1, 3):
        wait_y(dj)

    raw[...] = recv2[y_owner]
    halo_after = remote(raw, halo.at[0], h_send.at[0], h_recv.at[0], (dp, after))
    halo_before = remote(raw, halo.at[1], h_send.at[1], h_recv.at[1], (dp, before))
    halo_after.start()
    halo_before.start()

    for g in range(depth):
        field[0, depth + g] = raw[:, g * plane : (g + 1) * plane].astype(f32)
    position = lax.broadcasted_iota(jnp.int32, (PIECE, plane), 1)
    column = lax.rem(position, WIDTH_Y)
    sweeps = table_ref.shape[0]

    def smooth(k, l):
        u = field[k, l]
        north = jnp.where(position >= WIDTH_Y, pltpu.roll(u, WIDTH_Y, 1), 0.0)
        south = jnp.where(position < plane - WIDTH_Y, pltpu.roll(u, plane - WIDTH_Y, 1), 0.0)
        west = jnp.where(column > 0, pltpu.roll(u, 1, 1), 0.0)
        east = jnp.where(column < WIDTH_Y - 1, pltpu.roll(u, plane - 1, 1), 0.0)
        e = l - depth + 2
        updated = (
            coef[k, 0, e : e + 1] * u
            + coef[k, 1, e : e + 1] * ((north + south) + (west + east))
            + coef[k, 2, e : e + 1] * field[k, l - 1]
            + coef[k, 3, e : e + 1] * field[k, l + 1]
        )
        if k + 1 < sweeps:
            field[k + 1, l] = updated
        else:
            g = l - depth
            gath[x, 0, :, g * plane : (g + 1) * plane] = updated.astype(bf16)

    def copy_g5(dj):
        return remote(
            gath.at[x, 0], gath.at[x, 4 - dj], g5_send.at[dj], g5_recv.at[4 - dj], at(x, lax.rem(yh + dj, 4), me)
        )

    def wait_g5(dj):
        remote(gath.at[x, 0], gath.at[x, dj], g5_send.at[dj], g5_recv.at[dj], at(right, yh, me)).wait_recv()

    def copy_g6(way, source, first, last, slot):
        part_of = gath.at[source, first:last]
        return remote(part_of, part_of, g6_send.at[slot], g6_recv.at[slot], at(way, yh, me))

    to_right = [copy_g6(right, x, 0, 1, 0), copy_g6(right, x, 1, 4, 1), copy_g6(right, left, 0, 2, 2)]
    to_left = [copy_g6(left, x, 0, 1, 3), copy_g6(left, x, 1, 4, 4), copy_g6(left, right, 2, 4, 5)]
    far = lax.rem(x + 2, 4)
    from_left = [copy_g6(right, left, 0, 1, 0), copy_g6(right, left, 1, 4, 1), copy_g6(right, far, 0, 2, 2)]
    from_right = [copy_g6(left, right, 0, 1, 3), copy_g6(left, right, 1, 4, 4), copy_g6(left, far, 2, 4, 5)]

    inner = [(0, l) for l in range(depth + 1, 2 * depth - 1)]
    done = set(inner)
    for k, l in inner:
        smooth(k, l)

    halo_after.wait_recv()
    halo_before.wait_recv()
    has_before = jnp.where(me > 0, 1.0, 0.0).astype(f32)
    has_after = jnp.where(me < slabs - 1, 1.0, 0.0).astype(f32)
    for g in range(depth):
        cut = slice(g * plane, (g + 1) * plane)
        field[0, g] = halo[0, :, cut].astype(f32) * has_before
        field[0, 2 * depth + g] = halo[1, :, cut].astype(f32) * has_after

    def smooth_all(k, l):
        if k < 0 or (k, l) in done:
            return
        for near in (l - 1, l, l + 1):
            smooth_all(k - 1, near)
        smooth(k, l)
        done.add((k, l))

    for t in range(depth):
        smooth_all(sweeps - 1, depth + t)
    for dj in (2, 1, 3):
        copy_g5(dj).start()
    to_right[0].start()
    to_left[0].start()
    for dj in (1, 3, 2):
        wait_g5(dj)
    to_right[1].start()
    to_left[1].start()

    def into_panel(source):
        rows = gath[source].astype(f32).reshape(GROUP, cells).astype(bf16)
        panel[pl.ds(pl.multiple_of(source * GROUP, GROUP), GROUP)] = rows

    into_panel(x)
    from_left[0].wait_recv()
    from_right[0].wait_recv()
    from_left[1].wait_recv()
    to_right[2].start()
    from_right[1].wait_recv()
    to_left[2].start()
    into_panel(left)
    into_panel(right)
    from_left[2].wait_recv()
    from_right[2].wait_recv()
    into_panel(far)

    data_rows = groups * GROUP
    chunk = min(CHUNK, data_rows)
    chunks = data_rows // chunk
    blocks = chunk // (2 * out_rows)
    own_chunk = lax.div(chip, blocks)

    def copy_sibling(turn):
        return remote(
            product.at[turn, 1 - core], sibling_in.at[turn], sib_send.at[turn], sib_recv.at[turn], (dp, sibling)
        )

    def copy_part(to):
        return remote(part.at[to], parts_in.at[chip], rs_send.at[0], rs_recv.at[0], (dp, 2 * to + core))

    def chunk_of(turn):
        return lax.rem(own_chunk + 1 + turn, chunks)

    def multiply(turn):
        here = chunk_of(turn)
        rows = sens[pl.ds(here * (chunk // GROUP), chunk // GROUP)].reshape(chunk, cells)
        result = lax.dot_general(rows, panel[...], (((1,), (1,)), ((), ())), preferred_element_type=f32)
        result = result.reshape(blocks, 2, out_rows, PANEL)
        for half in range(2):
            product[turn, half] = result[:, half]
        copy_sibling(turn).start()

    def send_parts(turn):
        here = chunk_of(turn)
        copy_sibling(turn).wait_recv()
        part[pl.ds(here * blocks, blocks)] = (product[turn, core] + sibling_in[turn]).astype(bf16)
        for i in range(blocks):
            to = here * blocks + i

            @pl.when(to != chip)
            def _(to=to):
                copy_part(to).start()

    for turn in range(chunks):
        multiply(turn)
        if turn > 0:
            send_parts(turn - 1)
    send_parts(chunks - 1)
    parts_in[chip] = part[chip]

    class_after.wait_send()
    class_before.wait_send()
    halo_after.wait_send()
    halo_before.wait_send()

    @pl.when(x < 2)
    def _():
        for copy in (copy_far, copy_in, copy_mate, copy_out, copy_in_late, copy_chosen):
            copy.wait_send()

    @pl.when(x >= 2)
    def _():
        copy_on.wait_send()

    for dj in (1, 2, 3):
        copy_y(dj).wait_send()
        copy_g5(dj).wait_send()
    for copy in to_right + to_left:
        copy.wait_send()
    for turn in range(chunks):
        copy_sibling(turn).wait_send()

    others = remote(
        part.at[0 : chips - 1], parts_in.at[0 : chips - 1], rs_send.at[0], rs_recv.at[0], (dp, sibling)
    )
    others.wait_send()
    others.wait_recv()

    total = jnp.zeros(out_ref.shape, f32)
    for i in range(chips):
        total = total + parts_in[i].astype(f32)
    total = total * (1.0 / math.sqrt(layers * plane))
    col = lax.broadcasted_iota(jnp.int32, out_ref.shape, 1)
    shift = PIECE * yh
    total = jnp.where(
        lax.rem(col, GROUP) >= shift,
        pltpu.roll(total, shift, 1),
        pltpu.roll(total, shift + PANEL - GROUP, 1),
    )
    base = dp * data_rows + me * out_rows
    row = base + lax.broadcasted_iota(jnp.int32, out_ref.shape, 0)
    out_ref[...] = jnp.where(row >= start * PANEL + col, total, 0.0)


def body(sensitivity, panel_index, cell_class, tear_layer, coef_table):
    rows, cells = sensitivity.shape
    depth, plane = cell_class.shape
    slabs = lax.axis_size("slab")
    out_rows = rows // slabs
    groups = rows // GROUP
    chips = slabs // 2
    chunks = max(1, rows // CHUNK)
    bf16 = jnp.bfloat16
    dma = pltpu.SemaphoreType.DMA
    sweeps = coef_table.shape[0]
    ext = -(-(depth + 4) // 8) * 8
    return pl.pallas_call(
        functools.partial(kernel, slabs),
        out_shape=jax.ShapeDtypeStruct((out_rows, PANEL), jnp.float32),
        in_specs=[pl.BlockSpec(memory_space=pltpu.HBM)] * 5,
        out_specs=pl.BlockSpec(memory_space=pltpu.VMEM),
        scratch_shapes=[
            pltpu.SMEM(panel_index.shape, jnp.int32),
            pltpu.SMEM(coef_table.shape, jnp.float32),
            pltpu.VMEM((depth, plane), jnp.int32),
            pltpu.VMEM((1, plane), jnp.int32),
            pltpu.VMEM((groups, GROUP, cells), bf16),
            pltpu.VMEM((4, 4, PIECE, cells), bf16),
            pltpu.VMEM((2, 2, PIECE, cells), bf16),
            pltpu.VMEM((2, 2, PIECE, cells), bf16),
            pltpu.VMEM((2, PIECE, cells), bf16),
            pltpu.VMEM((2, 2, PIECE, cells), bf16),
            pltpu.VMEM((2, PIECE, cells), bf16),
            pltpu.VMEM((4, PIECE, cells), bf16),
            pltpu.VMEM((4, PIECE, cells), bf16),
            pltpu.VMEM((PIECE, cells), bf16),
            pltpu.VMEM((2, PIECE, cells), bf16),
            pltpu.VMEM((2, depth, plane), jnp.int32),
            pltpu.VMEM((ext, plane), jnp.int32),
            pltpu.VMEM((sweeps, 4, ext, plane), jnp.float32),
            pltpu.VMEM((sweeps, 3 * depth, PIECE, plane), jnp.float32),
            pltpu.VMEM((4, 4, PIECE, cells), bf16),
            pltpu.VMEM((PANEL, cells), bf16),
            pltpu.VMEM((chunks, 2, rows // chunks // (2 * out_rows), out_rows, PANEL), jnp.float32),
            pltpu.VMEM((chunks, rows // chunks // (2 * out_rows), out_rows, PANEL), jnp.float32),
            pltpu.VMEM((chips, out_rows, PANEL), bf16),
            pltpu.VMEM((chips, out_rows, PANEL), bf16),
            dma((5,)),
            dma((2,)),
            dma((2,)),
            dma((6,)),
            dma((6,)),
            dma((4,)),
            dma((4,)),
            dma((2,)),
            dma((2,)),
            dma((4,)),
            dma((4,)),
            dma((6,)),
            dma((6,)),
            dma((chunks,)),
            dma((chunks,)),
            dma((1,)),
            dma((1,)),
        ],
        compiler_params=pltpu.CompilerParams(
            collective_id=0, has_side_effects=True, vmem_limit_bytes=VMEM_LIMIT
        ),
        cost_estimate=pl.CostEstimate(
            flops=2 * rows * cells * PANEL, bytes_accessed=2 * rows * cells, transcendentals=0
        ),
        name="panel",
    )(
        panel_index,
        coef_table,
        sensitivity.reshape(groups, GROUP, cells),
        cell_class,
        tear_layer.reshape(1, plane),
    )


def solution(mesh):
    return jax.shard_map(
        body,
        mesh=mesh,
        in_specs=(P("dp", "slab"), P(), P("slab", None), P(), P()),
        out_specs=P(("dp", "slab"), None),
        check_vma=False,
    )
```

time: 663 us -> 58.3 us (0.09)
  waiting for transfers between devices: 419 us -> 0 us
  other arithmetic: 153 us -> 0 us
  Pallas kernels: 0 us -> 56 us
  local copies, waits for them, and re-layouts: 43 us -> 1.31 us
  starting transfers between devices: 23.9 us -> 0 us
  between operations: 15 us -> 0.66 us
    unnamed x3 -> x0, waiting for transfers between devices: 220 us -> none
    psum x1 -> x0, waiting for transfers between devices: 170 us -> none  [spread(): return lax.psum(block, axis)]
    select_n x14 -> x0, other arithmetic: 62.7 us -> none  [the longest x12 60.7 us: sweep(): coef_h = jnp.where(inner == level, coef_table[number, 0, level], coef_h)]
    mul x12 -> x0, other arithmetic: 61.1 us -> none  [sweep(): 4.0 * coef_v * vertical]
    pallas_call x0 -> x1, Pallas kernels: none -> 56 us  [body(): pl.pallas_call(functools.partial(kernel, slabs), out_shape=jax.ShapeDtype...]
    ppermute x6 -> x0, waiting for transfers between devices: 29.5 us -> none  [the longest x3 22.4 us: padded_2(): lax.ppermute(lax.slice_in_dim(block, 0, width, axis=dim), axis, backward)]
    ppermute x6 -> x0, starting transfers between devices: 23.9 us -> none  [the longest x3 16.9 us: padded_2(): lax.ppermute(lax.slice_in_dim(block, block.shape[dim] - width, None, axis...]
    dynamic_update_slice x12 -> x0, other arithmetic: 16.4 us -> none  [blockwise(): result = lax.map(action, stacked)]
  transfers between devices with their start and end apart: 8 -> 0, of which waited for: 7 -> 0; matrix products, arithmetic and copies ran while one was open for 1% -> 0% of each run, Pallas kernels for 0% -> 0%
where the time goes in v1:
time: 58.3 us; the launch traced here: 58 us
  Pallas kernels  56 us (96%)
  local copies, waits for them, and re-layouts  1.31 us (2%)
  between operations  0.66 us (1%)
    pallas_call x1, Pallas kernels, body(): pl.pallas_call(functools.partial(kernel, slabs), out_shape=jax.ShapeDtype...  56 us
    unnamed x1, local copies, waits for them, and re-layouts  1.31 us

profile of v1, /device:TPU:1, one launch (start us, length us, event | category | flops | bytes accessed | tf_op | source)
XLA Modules:
  0.0 58.0 jit_solution(3358333995383064196)
XLA Ops:
  0.7 56.0 %panel.1 = f32[24,128]{1,0:T(8,128)} custom-call(s32[1]{0:T(128)S(6)} %copy.7.panel_hbm, f32[3,2,8]{2,1,0:T(2,128)} %table_hbm.1, bf16[24,32,3072]{2,1,0:T(8,128)(2,1)} %bitcast.2, s32[3,1024]{1,0:T(4,128)} %class_hbm.1, s32[1,1024]{1,0:T(1,128)} %bitcast.3), custom_call_target="tpu_custom_call" | custom-call | flops 603979776 | bytes 4718592 | tf_op jit(solution)/shard_map/panel/pallas_call | solution.py:456
  56.7 1.3 %copy.8 = f32[24,128]{1,0:T(8,128)} copy(f32[24,128]{1,0:T(8,128)} %panel.1) | data formatting | bytes 24576

commit v2 on v1

--- a/solution.py
+++ b/solution.py
@@ -181,7 +181,7 @@
 
     @pl.when(x < 2)
     def _():
-        for copy in (copy_far, copy_in, copy_mate, copy_out, copy_in_late):
+        for copy in (copy_far, copy_mate, copy_in, copy_out, copy_in_late):
             copy.start()
         recv_early[x] = send1[x, 0:2]
         recv_late[x] = send1[x, 2:4]
@@ -285,23 +285,27 @@
             g = l - depth
             gath[x, 0, :, g * plane : (g + 1) * plane] = updated.astype(bf16)
 
-    def copy_g5(dj):
-        return remote(
-            gath.at[x, 0], gath.at[x, 4 - dj], g5_send.at[dj], g5_recv.at[4 - dj], at(x, lax.rem(yh + dj, 4), me)
-        )
-
-    def wait_g5(dj):
-        remote(gath.at[x, 0], gath.at[x, dj], g5_send.at[dj], g5_recv.at[dj], at(right, yh, me)).wait_recv()
+    def copy_g5(place, dj, lands):
+        target = at(x, lax.rem(yh + dj, 4), me)
+        return remote(gath.at[x, 0], gath.at[x, lands], g5_send.at[place], g5_recv.at[lands], target)
+
+    over_y = [copy_g5(3, 2, 3), copy_g5(1, 1, 2), copy_g5(2, 3, 1)]
+
+    def wait_g5(place):
+        remote(gath.at[x, 0], gath.at[x, place], g5_send.at[place], g5_recv.at[place], at(right, yh, me)).wait_recv()
 
     def copy_g6(way, source, first, last, slot):
         part_of = gath.at[source, first:last]
         return remote(part_of, part_of, g6_send.at[slot], g6_recv.at[slot], at(way, yh, me))
 
-    to_right = [copy_g6(right, x, 0, 1, 0), copy_g6(right, x, 1, 4, 1), copy_g6(right, left, 0, 2, 2)]
-    to_left = [copy_g6(left, x, 0, 1, 3), copy_g6(left, x, 1, 4, 4), copy_g6(left, right, 2, 4, 5)]
+    rounds = [(0, 1), (1, 3), (3, 4)]
     far = lax.rem(x + 2, 4)
-    from_left = [copy_g6(right, left, 0, 1, 0), copy_g6(right, left, 1, 4, 1), copy_g6(right, far, 0, 2, 2)]
-    from_right = [copy_g6(left, right, 0, 1, 3), copy_g6(left, right, 1, 4, 4), copy_g6(left, far, 2, 4, 5)]
+    to_right = [copy_g6(right, x, *span, i) for i, span in enumerate(rounds)]
+    to_left = [copy_g6(left, x, *span, 3 + i) for i, span in enumerate(rounds)]
+    from_left = [copy_g6(right, left, *span, i) for i, span in enumerate(rounds)]
+    from_right = [copy_g6(left, right, *span, 3 + i) for i, span in enumerate(rounds)]
+    relays = [copy_g6(right, left, 0, 2, 6), copy_g6(left, right, 2, 3, 7), copy_g6(left, right, 3, 4, 8)]
+    relayed = [copy_g6(right, far, 0, 2, 6), copy_g6(left, far, 2, 3, 7), copy_g6(left, far, 3, 4, 8)]
 
     inner = [(0, l) for l in range(depth + 1, 2 * depth - 1)]
     done = set(inner)
@@ -327,30 +331,34 @@
 
     for t in range(depth):
         smooth_all(sweeps - 1, depth + t)
-    for dj in (2, 1, 3):
-        copy_g5(dj).start()
-    to_right[0].start()
-    to_left[0].start()
-    for dj in (1, 3, 2):
-        wait_g5(dj)
-    to_right[1].start()
-    to_left[1].start()
+    for copy in over_y + [to_right[0], to_left[0]]:
+        copy.start()
 
     def into_panel(source):
         rows = gath[source].astype(f32).reshape(GROUP, cells).astype(bf16)
         panel[pl.ds(pl.multiple_of(source * GROUP, GROUP), GROUP)] = rows
 
+    wait_g5(1)
+    wait_g5(2)
+    to_right[1].start()
+    to_left[1].start()
+    wait_g5(3)
+    to_right[2].start()
+    to_left[2].start()
+    from_left[0].wait_recv()
+    from_left[1].wait_recv()
+    relays[0].start()
+    from_right[0].wait_recv()
+    from_right[1].wait_recv()
+    relays[1].start()
+    from_right[2].wait_recv()
+    relays[2].start()
     into_panel(x)
-    from_left[0].wait_recv()
-    from_right[0].wait_recv()
-    from_left[1].wait_recv()
-    to_right[2].start()
-    from_right[1].wait_recv()
-    to_left[2].start()
-    into_panel(left)
     into_panel(right)
     from_left[2].wait_recv()
-    from_right[2].wait_recv()
+    into_panel(left)
+    for copy in relayed:
+        copy.wait_recv()
     into_panel(far)
 
     data_rows = groups * GROUP
@@ -413,8 +421,7 @@
 
     for dj in (1, 2, 3):
         copy_y(dj).wait_send()
-        copy_g5(dj).wait_send()
-    for copy in to_right + to_left:
+    for copy in over_y + to_right + to_left + relays:
         copy.wait_send()
     for turn in range(chunks):
         copy_sibling(turn).wait_send()
@@ -430,6 +437,10 @@
         total = total + parts_in[i].astype(f32)
     total = total * (1.0 / math.sqrt(layers * plane))
     col = lax.broadcasted_iota(jnp.int32, out_ref.shape, 1)
+    place = lax.div(lax.rem(col, GROUP), PIECE)
+    total = jnp.where(
+        place == 2, pltpu.roll(total, PANEL - PIECE, 1), jnp.where(place == 3, pltpu.roll(total, PIECE, 1), total)
+    )
     shift = PIECE * yh
     total = jnp.where(
         lax.rem(col, GROUP) >= shift,
@@ -495,8 +506,8 @@
             dma((2,)),
             dma((4,)),
             dma((4,)),
-            dma((6,)),
-            dma((6,)),
+            dma((9,)),
+            dma((9,)),
             dma((chunks,)),
             dma((chunks,)),
             dma((1,)),

time: 58.3 us -> 57.3 us (0.983)
  Pallas kernels: 56 us -> 55.1 us
    pallas_call x1, Pallas kernels: 56 us -> 55.1 us  [body(): pl.pallas_call(functools.partial(kernel, slabs), out_shape=jax.ShapeDtype...]
where the time goes in v2:
time: 57.3 us; the launch traced here: 57.1 us
  Pallas kernels  55.1 us (96%)
  local copies, waits for them, and re-layouts  1.31 us (2%)
  between operations  0.66 us (1%)
    pallas_call x1, Pallas kernels, body(): pl.pallas_call(functools.partial(kernel, slabs), out_shape=jax.ShapeDtype...  55.1 us
    unnamed x1, local copies, waits for them, and re-layouts  1.31 us

profile of v2, /device:TPU:1, one launch (start us, length us, event | category | flops | bytes accessed | tf_op | source)
XLA Modules:
  0.0 57.1 jit_solution(17607450755334476228)
XLA Ops:
  0.7 55.1 %panel.1 = f32[24,128]{1,0:T(8,128)} custom-call(s32[1]{0:T(128)S(6)} %copy.7.panel_hbm, f32[3,2,8]{2,1,0:T(2,128)} %table_hbm.1, bf16[24,32,3072]{2,1,0:T(8,128)(2,1)} %bitcast.2, s32[3,1024]{1,0:T(4,128)} %class_hbm.1, s32[1,1024]{1,0:T(1,128)} %bitcast.3), custom_call_target="tpu_custom_call" | custom-call | flops 603979776 | bytes 4718592 | tf_op jit(solution)/shard_map/panel/pallas_call | solution.py:467
  55.7 1.3 %copy.8 = f32[24,128]{1,0:T(8,128)} copy(f32[24,128]{1,0:T(8,128)} %panel.1) | data formatting | bytes 24576

commit v3 on v2

--- a/solution.py
+++ b/solution.py
@@ -11,6 +11,7 @@
 WIDTH_Y = 32
 PANEL = 128
 GROUP = 32
+HALF = 16
 PIECE = 8
 CHUNK = 384
 VMEM_LIMIT = 63 * 1024 * 1024
@@ -124,17 +125,16 @@
             barrier, inc=1, device_id=target, device_id_type=pl.DeviceIdType.MESH
         )
 
+    for d in sorted(range(1, chips), key=lambda d: -min(d, chips - d)):
+        greet((dp, lax.rem(me + 2 * d, slabs)))
+
+    for dj in (2, 1, 3):
+        greet(at(x, lax.rem(yh + dj, 4), me))
+    greet((dp, before))
+    greet((dp, after))
     greet(at(right, yh, me))
     greet(at(left, yh, me))
-    for dj in (1, 2, 3):
-        greet(at(x, lax.rem(yh + dj, 4), me))
-
-    greet((dp, before))
-    greet((dp, after))
-
-    @pl.loop(1, chips)
-    def _(d):
-        greet((dp, lax.rem(me + 2 * d, slabs)))
+    greet(at(lax.rem(x + 2, 4), yh, me))
 
     for copy in small:
         copy.wait()
@@ -149,22 +149,15 @@
     @pl.when(x < 2)
     def _():
         for q in range(4):
-            rows = sens[first_group + q].astype(f32).reshape(4, PIECE, cells).astype(bf16)
-            for j in range(4):
-                send1[q, lax.rem(j - yh + 6, 4)] = rows[j]
-
-    pl.semaphore_wait(barrier, 7 + chips - 1)
-
-    class_after = remote(class_ref, class_halo.at[0], class_send.at[0], class_recv.at[0], (dp, after))
-    class_before = remote(class_ref, class_halo.at[1], class_send.at[1], class_recv.at[1], (dp, before))
-    class_after.start()
-    class_before.start()
+            send1[q] = sens[first_group + q].reshape(2, HALF, cells)
+
+    pl.semaphore_wait(barrier, 8 + chips - 1)
 
     def early(q):
-        return send1.at[q, 0:2]
+        return send1.at[q, 0]
 
     def late(q):
-        return send1.at[q, 2:4]
+        return send1.at[q, 1]
 
     mate = at(1 - x, yh, me)
     outer = at(3 - x, yh, me)
@@ -183,9 +176,14 @@
     def _():
         for copy in (copy_far, copy_mate, copy_in, copy_out, copy_in_late):
             copy.start()
-        recv_early[x] = send1[x, 0:2]
-        recv_late[x] = send1[x, 2:4]
-        pair1[x] = send1[3 - x, 2:4]
+        recv_early[x] = send1[x, 0]
+        recv_late[x] = send1[x, 1]
+        pair1[x] = send1[3 - x, 1]
+
+    class_after = remote(class_ref, class_halo.at[0], class_send.at[0], class_recv.at[0], (dp, after))
+    class_before = remote(class_ref, class_halo.at[1], class_send.at[1], class_recv.at[1], (dp, before))
+    class_after.start()
+    class_before.start()
 
     class_after.wait_recv()
     class_before.wait_recv()
@@ -214,14 +212,25 @@
         coef[k, 2] = up
         coef[k, 3] = down
 
-    def copy_y(dj):
-        return remote(
-            send2.at[dj], recv2.at[yh], s2_send.at[dj], s2_recv.at[yh], at(x, lax.rem(yh + dj, 4), me)
-        )
+    def copy_y(j):
+        return remote(send2.at[j], recv2.at[yh], s2_send.at[j], s2_recv.at[yh], at(x, j, me))
 
     def wait_y(dj):
         j = lax.rem(yh + dj, 4)
-        remote(send2.at[dj], recv2.at[j], s2_send.at[dj], s2_recv.at[j], at(x, j, me)).wait_recv()
+        remote(send2.at[j], recv2.at[j], s2_send.at[j], s2_recv.at[j], at(x, j, me)).wait_recv()
+
+    def scatter_y(rows, first):
+        pieces = rows.astype(f32).reshape(2, PIECE, cells).astype(bf16)
+        for j in (first, first + 1):
+
+            @pl.when(yh == j)
+            def _(j=j):
+                recv2[yh] = pieces[j - first]
+
+            @pl.when(yh != j)
+            def _(j=j):
+                send2[j] = pieces[j - first]
+                copy_y(j).start()
 
     @pl.when(x >= 2)
     def _():
@@ -230,11 +239,7 @@
         arrived(3, recv_early.at[3 - x])
 
     arrived(1, recv_early.at[jnp.where(x < 2, 1 - x, x - 2)])
-    chosen = recv_early[x_owner]
-    send2[2] = chosen[0]
-    copy_y(2).start()
-    send2[3] = chosen[1]
-    copy_y(3).start()
+    scatter_y(recv_early[x_owner], 0)
 
     @pl.when(x < 2)
     def _():
@@ -247,10 +252,7 @@
     def _():
         arrived(5, recv_late.at[0])
 
-    chosen = recv_late[jnp.where(x < 2, x_owner, 0)]
-    send2[1] = chosen[1]
-    copy_y(1).start()
-    recv2[yh] = chosen[0]
+    scatter_y(recv_late[jnp.where(x < 2, x_owner, 0)], 2)
     for dj in (2, 1, 3):
         wait_y(dj)
 
@@ -304,8 +306,9 @@
     to_left = [copy_g6(left, x, *span, 3 + i) for i, span in enumerate(rounds)]
     from_left = [copy_g6(right, left, *span, i) for i, span in enumerate(rounds)]
     from_right = [copy_g6(left, right, *span, 3 + i) for i, span in enumerate(rounds)]
-    relays = [copy_g6(right, left, 0, 2, 6), copy_g6(left, right, 2, 3, 7), copy_g6(left, right, 3, 4, 8)]
-    relayed = [copy_g6(right, far, 0, 2, 6), copy_g6(left, far, 2, 3, 7), copy_g6(left, far, 3, 4, 8)]
+    relays = [copy_g6(right, left, 0, 2, 6), copy_g6(left, right, 2, 3, 7)]
+    to_far = copy_g6(far, x, 3, 4, 8)
+    relayed = [copy_g6(right, far, 0, 2, 6), copy_g6(left, far, 2, 3, 7), copy_g6(far, far, 3, 4, 8)]
 
     inner = [(0, l) for l in range(depth + 1, 2 * depth - 1)]
     done = set(inner)
@@ -343,6 +346,7 @@
     to_right[1].start()
     to_left[1].start()
     wait_g5(3)
+    to_far.start()
     to_right[2].start()
     to_left[2].start()
     from_left[0].wait_recv()
@@ -351,9 +355,8 @@
     from_right[0].wait_recv()
     from_right[1].wait_recv()
     relays[1].start()
+    into_panel(x)
     from_right[2].wait_recv()
-    relays[2].start()
-    into_panel(x)
     into_panel(right)
     from_left[2].wait_recv()
     into_panel(left)
@@ -419,9 +422,13 @@
     def _():
         copy_on.wait_send()
 
-    for dj in (1, 2, 3):
-        copy_y(dj).wait_send()
-    for copy in over_y + to_right + to_left + relays:
+    for j in range(4):
+
+        @pl.when(yh != j)
+        def _(j=j):
+            copy_y(j).wait_send()
+
+    for copy in over_y + to_right + to_left + relays + [to_far]:
         copy.wait_send()
     for turn in range(chunks):
         copy_sibling(turn).wait_send()
@@ -475,12 +482,12 @@
             pltpu.VMEM((depth, plane), jnp.int32),
             pltpu.VMEM((1, plane), jnp.int32),
             pltpu.VMEM((groups, GROUP, cells), bf16),
-            pltpu.VMEM((4, 4, PIECE, cells), bf16),
-            pltpu.VMEM((2, 2, PIECE, cells), bf16),
-            pltpu.VMEM((2, 2, PIECE, cells), bf16),
-            pltpu.VMEM((2, PIECE, cells), bf16),
-            pltpu.VMEM((2, 2, PIECE, cells), bf16),
-            pltpu.VMEM((2, PIECE, cells), bf16),
+            pltpu.VMEM((4, 2, HALF, cells), bf16),
+            pltpu.VMEM((2, HALF, cells), bf16),
+            pltpu.VMEM((2, HALF, cells), bf16),
+            pltpu.VMEM((HALF, cells), bf16),
+            pltpu.VMEM((2, HALF, cells), bf16),
+            pltpu.VMEM((HALF, cells), bf16),
             pltpu.VMEM((4, PIECE, cells), bf16),
             pltpu.VMEM((4, PIECE, cells), bf16),
             pltpu.VMEM((PIECE, cells), bf16),

time: 57.3 us -> 58.6 us (1.023)
  Pallas kernels: 55.1 us -> 56.4 us
    pallas_call x1, Pallas kernels: 55.1 us -> 56.4 us  [body(): pl.pallas_call(functools.partial(kernel, slabs), out_shape=jax.ShapeDtype...]
where the time goes in v3:
time: 58.6 us; the launch traced here: 58.4 us
  Pallas kernels  56.4 us (96%)
  local copies, waits for them, and re-layouts  1.31 us (2%)
  between operations  0.66 us (1%)
    pallas_call x1, Pallas kernels, body(): pl.pallas_call(functools.partial(kernel, slabs), out_shape=jax.ShapeDtype...  56.4 us
    unnamed x1, local copies, waits for them, and re-layouts  1.31 us

profile of v3, /device:TPU:1, one launch (start us, length us, event | category | flops | bytes accessed | tf_op | source)
XLA Modules:
  0.0 58.4 jit_solution(2929804365871426310)
XLA Ops:
  0.7 56.4 %panel.1 = f32[24,128]{1,0:T(8,128)} custom-call(s32[1]{0:T(128)S(6)} %copy.7.panel_hbm, f32[3,2,8]{2,1,0:T(2,128)} %table_hbm.1, bf16[24,32,3072]{2,1,0:T(8,128)(2,1)} %bitcast.2, s32[3,1024]{1,0:T(4,128)} %class_hbm.1, s32[1,1024]{1,0:T(1,128)} %bitcast.3), custom_call_target="tpu_custom_call" | custom-call | flops 603979776 | bytes 4718592 | tf_op jit(solution)/shard_map/panel/pallas_call | solution.py:474
  57.0 1.3 %copy.8 = f32[24,128]{1,0:T(8,128)} copy(f32[24,128]{1,0:T(8,128)} %panel.1) | data formatting | bytes 24576

commit v4 on v3

--- a/solution.py
+++ b/solution.py
@@ -49,7 +49,6 @@
     product,
     sibling_in,
     part,
-    parts_in,
     load_sem,
     class_send,
     class_recv,
@@ -81,7 +80,7 @@
     sibling = me + 1 - 2 * core
     depth, plane = class_ref.shape
     layers = depth * slabs
-    out_rows = out_ref.shape[0]
+    out_rows = out_ref.shape[1]
     panels_dev = groups * GROUP // PANEL
     right = lax.rem(x + 1, 4)
     left = lax.rem(x + 3, 4)
@@ -134,7 +133,6 @@
     greet((dp, after))
     greet(at(right, yh, me))
     greet(at(left, yh, me))
-    greet(at(lax.rem(x + 2, 4), yh, me))
 
     for copy in small:
         copy.wait()
@@ -151,7 +149,7 @@
         for q in range(4):
             send1[q] = sens[first_group + q].reshape(2, HALF, cells)
 
-    pl.semaphore_wait(barrier, 8 + chips - 1)
+    pl.semaphore_wait(barrier, 7 + chips - 1)
 
     def early(q):
         return send1.at[q, 0]
@@ -239,7 +237,22 @@
         arrived(3, recv_early.at[3 - x])
 
     arrived(1, recv_early.at[jnp.where(x < 2, 1 - x, x - 2)])
+    halo_after = remote(raw, halo.at[0], h_send.at[0], h_recv.at[0], (dp, after))
+    halo_before = remote(raw, halo.at[1], h_send.at[1], h_recv.at[1], (dp, before))
+
+    def start_halo():
+        for dj in (1, 2, 3):
+            wait_y(dj)
+        raw[...] = recv2[y_owner]
+        halo_after.start()
+        halo_before.start()
+
     scatter_y(recv_early[x_owner], 0)
+
+    @pl.when(yh < 2)
+    def _():
+        start_halo()
+
 
     @pl.when(x < 2)
     def _():
@@ -253,14 +266,9 @@
         arrived(5, recv_late.at[0])
 
     scatter_y(recv_late[jnp.where(x < 2, x_owner, 0)], 2)
-    for dj in (2, 1, 3):
-        wait_y(dj)
-
-    raw[...] = recv2[y_owner]
-    halo_after = remote(raw, halo.at[0], h_send.at[0], h_recv.at[0], (dp, after))
-    halo_before = remote(raw, halo.at[1], h_send.at[1], h_recv.at[1], (dp, before))
-    halo_after.start()
-    halo_before.start()
+    @pl.when(yh >= 2)
+    def _():
+        start_halo()
 
     for g in range(depth):
         field[0, depth + g] = raw[:, g * plane : (g + 1) * plane].astype(f32)
@@ -285,30 +293,58 @@
             field[k + 1, l] = updated
         else:
             g = l - depth
-            gath[x, 0, :, g * plane : (g + 1) * plane] = updated.astype(bf16)
-
-    def copy_g5(place, dj, lands):
-        target = at(x, lax.rem(yh + dj, 4), me)
-        return remote(gath.at[x, 0], gath.at[x, lands], g5_send.at[place], g5_recv.at[lands], target)
-
-    over_y = [copy_g5(3, 2, 3), copy_g5(1, 1, 2), copy_g5(2, 3, 1)]
-
-    def wait_g5(place):
-        remote(gath.at[x, 0], gath.at[x, place], g5_send.at[place], g5_recv.at[place], at(right, yh, me)).wait_recv()
+            gath[x, yh, :, g * plane : (g + 1) * plane] = updated.astype(bf16)
+
+    def copy_g5(dj):
+        own = gath.at[x, yh]
+        return remote(own, own, g5_send.at[dj], g5_recv.at[yh], at(x, lax.rem(yh + dj, 4), me))
+
+    over_y = [copy_g5(dj) for dj in (2, 1, 3)]
+
+    def wait_g5(j):
+        @pl.when(yh != j)
+        def _():
+            piece = gath.at[x, j]
+            remote(piece, piece, g5_send.at[0], g5_recv.at[j], at(right, yh, me)).wait_recv()
 
     def copy_g6(way, source, first, last, slot):
         part_of = gath.at[source, first:last]
         return remote(part_of, part_of, g6_send.at[slot], g6_recv.at[slot], at(way, yh, me))
 
-    rounds = [(0, 1), (1, 3), (3, 4)]
     far = lax.rem(x + 2, 4)
-    to_right = [copy_g6(right, x, *span, i) for i, span in enumerate(rounds)]
-    to_left = [copy_g6(left, x, *span, 3 + i) for i, span in enumerate(rounds)]
-    from_left = [copy_g6(right, left, *span, i) for i, span in enumerate(rounds)]
-    from_right = [copy_g6(left, right, *span, 3 + i) for i, span in enumerate(rounds)]
-    relays = [copy_g6(right, left, 0, 2, 6), copy_g6(left, right, 2, 3, 7)]
-    to_far = copy_g6(far, x, 3, 4, 8)
-    relayed = [copy_g6(right, far, 0, 2, 6), copy_g6(left, far, 2, 3, 7), copy_g6(far, far, 3, 4, 8)]
+
+    def gather_half(half):
+        first = 2 * half
+        wait_g5(first)
+        wait_g5(first + 1)
+        slot = 4 * half
+        sent = [
+            copy_g6(right, x, first, first + 2, slot),
+            copy_g6(left, x, first, first + 2, slot + 1),
+            copy_g6(right, left, first, first + 1, slot + 2),
+            copy_g6(left, right, first + 1, first + 2, slot + 3),
+        ]
+        sent[0].start()
+        sent[1].start()
+        into_panel(x, half)
+        copy_g6(right, left, first, first + 2, slot).wait_recv()
+        sent[2].start()
+        copy_g6(left, right, first, first + 2, slot + 1).wait_recv()
+        sent[3].start()
+        into_panel(left, half)
+        into_panel(right, half)
+        return sent
+
+    def gather_far(half):
+        first = 2 * half
+        slot = 4 * half
+        copy_g6(right, far, first, first + 1, slot + 2).wait_recv()
+        copy_g6(left, far, first + 1, first + 2, slot + 3).wait_recv()
+        into_panel(far, half)
+
+    def into_panel(source, half):
+        rows = gath[source, 2 * half : 2 * half + 2].astype(f32).reshape(HALF, cells).astype(bf16)
+        panel[pl.ds(pl.multiple_of(source * GROUP + half * HALF, HALF), HALF)] = rows
 
     inner = [(0, l) for l in range(depth + 1, 2 * depth - 1)]
     done = set(inner)
@@ -334,35 +370,12 @@
 
     for t in range(depth):
         smooth_all(sweeps - 1, depth + t)
-    for copy in over_y + [to_right[0], to_left[0]]:
+    for copy in over_y:
         copy.start()
-
-    def into_panel(source):
-        rows = gath[source].astype(f32).reshape(GROUP, cells).astype(bf16)
-        panel[pl.ds(pl.multiple_of(source * GROUP, GROUP), GROUP)] = rows
-
-    wait_g5(1)
-    wait_g5(2)
-    to_right[1].start()
-    to_left[1].start()
-    wait_g5(3)
-    to_far.start()
-    to_right[2].start()
-    to_left[2].start()
-    from_left[0].wait_recv()
-    from_left[1].wait_recv()
-    relays[0].start()
-    from_right[0].wait_recv()
-    from_right[1].wait_recv()
-    relays[1].start()
-    into_panel(x)
-    from_right[2].wait_recv()
-    into_panel(right)
-    from_left[2].wait_recv()
-    into_panel(left)
-    for copy in relayed:
-        copy.wait_recv()
-    into_panel(far)
+    over_x = gather_half(0)
+    over_x += gather_half(1)
+    gather_far(0)
+    gather_far(1)
 
     data_rows = groups * GROUP
     chunk = min(CHUNK, data_rows)
@@ -376,7 +389,7 @@
         )
 
     def copy_part(to):
-        return remote(part.at[to], parts_in.at[chip], rs_send.at[0], rs_recv.at[0], (dp, 2 * to + core))
+        return remote(part.at[to], out_ref.at[chip], rs_send.at[0], rs_recv.at[0], (dp, 2 * to + core))
 
     def chunk_of(turn):
         return lax.rem(own_chunk + 1 + turn, chunks)
@@ -393,7 +406,11 @@
     def send_parts(turn):
         here = chunk_of(turn)
         copy_sibling(turn).wait_recv()
-        part[pl.ds(here * blocks, blocks)] = (product[turn, core] + sibling_in[turn]).astype(bf16)
+        total = (product[turn, core] + sibling_in[turn]) * (1.0 / math.sqrt(layers * plane))
+        block = here * blocks + lax.broadcasted_iota(jnp.int32, total.shape, 0)
+        row = dp * data_rows + (2 * block + core) * out_rows + lax.broadcasted_iota(jnp.int32, total.shape, 1)
+        col = lax.broadcasted_iota(jnp.int32, total.shape, 2)
+        part[pl.ds(here * blocks, blocks)] = jnp.where(row >= start * PANEL + col, total, 0.0).astype(bf16)
         for i in range(blocks):
             to = here * blocks + i
 
@@ -406,7 +423,8 @@
         if turn > 0:
             send_parts(turn - 1)
     send_parts(chunks - 1)
-    parts_in[chip] = part[chip]
+    own_part = pltpu.make_async_copy(part.at[chip], out_ref.at[chip], rs_send.at[1])
+    own_part.start()
 
     class_after.wait_send()
     class_before.wait_send()
@@ -428,35 +446,17 @@
         def _(j=j):
             copy_y(j).wait_send()
 
-    for copy in over_y + to_right + to_left + relays + [to_far]:
+    for copy in over_y + over_x:
         copy.wait_send()
     for turn in range(chunks):
         copy_sibling(turn).wait_send()
 
     others = remote(
-        part.at[0 : chips - 1], parts_in.at[0 : chips - 1], rs_send.at[0], rs_recv.at[0], (dp, sibling)
+        part.at[0 : chips - 1], out_ref.at[0 : chips - 1], rs_send.at[0], rs_recv.at[0], (dp, sibling)
     )
     others.wait_send()
     others.wait_recv()
-
-    total = jnp.zeros(out_ref.shape, f32)
-    for i in range(chips):
-        total = total + parts_in[i].astype(f32)
-    total = total * (1.0 / math.sqrt(layers * plane))
-    col = lax.broadcasted_iota(jnp.int32, out_ref.shape, 1)
-    place = lax.div(lax.rem(col, GROUP), PIECE)
-    total = jnp.where(
-        place == 2, pltpu.roll(total, PANEL - PIECE, 1), jnp.where(place == 3, pltpu.roll(total, PIECE, 1), total)
-    )
-    shift = PIECE * yh
-    total = jnp.where(
-        lax.rem(col, GROUP) >= shift,
-        pltpu.roll(total, shift, 1),
-        pltpu.roll(total, shift + PANEL - GROUP, 1),
-    )
-    base = dp * data_rows + me * out_rows
-    row = base + lax.broadcasted_iota(jnp.int32, out_ref.shape, 0)
-    out_ref[...] = jnp.where(row >= start * PANEL + col, total, 0.0)
+    own_part.wait()
 
 
 def body(sensitivity, panel_index, cell_class, tear_layer, coef_table):
@@ -471,11 +471,11 @@
     dma = pltpu.SemaphoreType.DMA
     sweeps = coef_table.shape[0]
     ext = -(-(depth + 4) // 8) * 8
-    return pl.pallas_call(
+    parts = pl.pallas_call(
         functools.partial(kernel, slabs),
-        out_shape=jax.ShapeDtypeStruct((out_rows, PANEL), jnp.float32),
+        out_shape=jax.ShapeDtypeStruct((chips, out_rows, PANEL), bf16),
         in_specs=[pl.BlockSpec(memory_space=pltpu.HBM)] * 5,
-        out_specs=pl.BlockSpec(memory_space=pltpu.VMEM),
+        out_specs=pl.BlockSpec(memory_space=pltpu.HBM),
         scratch_shapes=[
             pltpu.SMEM(panel_index.shape, jnp.int32),
             pltpu.SMEM(coef_table.shape, jnp.float32),
@@ -501,7 +501,6 @@
             pltpu.VMEM((chunks, 2, rows // chunks // (2 * out_rows), out_rows, PANEL), jnp.float32),
             pltpu.VMEM((chunks, rows // chunks // (2 * out_rows), out_rows, PANEL), jnp.float32),
             pltpu.VMEM((chips, out_rows, PANEL), bf16),
-            pltpu.VMEM((chips, out_rows, PANEL), bf16),
             dma((5,)),
             dma((2,)),
             dma((2,)),
@@ -513,11 +512,11 @@
             dma((2,)),
             dma((4,)),
             dma((4,)),
-            dma((9,)),
-            dma((9,)),
+            dma((8,)),
+            dma((8,)),
             dma((chunks,)),
             dma((chunks,)),
-            dma((1,)),
+            dma((2,)),
             dma((1,)),
         ],
         compiler_params=pltpu.CompilerParams(
@@ -534,6 +533,7 @@
         cell_class,
         tear_layer.reshape(1, plane),
     )
+    return parts.astype(jnp.float32).sum(axis=0)
 
 
 def solution(mesh):

time: 58.6 us -> 64.4 us (1.099)
  Pallas kernels: 56.4 us -> 61.8 us
  other arithmetic: 0 us -> 1.51 us
  local copies, waits for them, and re-layouts: 1.31 us -> 0 us
    pallas_call x1, Pallas kernels: 56.4 us -> 61.8 us  [body(): pl.pallas_call(functools.partial(kernel, slabs), out_shape=jax.ShapeDtype...]
    reduce_sum x0 -> x1, other arithmetic: none -> 1.51 us  [body(): return parts.astype(jnp.float32).sum(axis=0)]
    unnamed x1 -> x0, local copies, waits for them, and re-layouts: 1.31 us -> none
where the time goes in v4:
time: 64.4 us; the launch traced here: 63.9 us
  Pallas kernels  61.8 us (96%)
  other arithmetic  1.51 us (2%)
  between operations  0.66 us (1%)
    pallas_call x1, Pallas kernels, body(): pl.pallas_call(functools.partial(kernel, slabs), out_shape=jax.ShapeDtype...  61.8 us
    reduce_sum x1, other arithmetic, body(): return parts.astype(jnp.float32).sum(axis=0)  1.51 us

profile of v4, /device:TPU:1, one launch (start us, length us, event | category | flops | bytes accessed | tf_op | source)
XLA Modules:
  0.0 63.9 jit_solution(14078415119192301598)
XLA Ops:
  0.7 61.8 %panel.1 = bf16[16,24,128]{2,1,0:T(8,128)(2,1)} custom-call(s32[1]{0:T(128)S(6)} %copy.6.panel_hbm, f32[3,2,8]{2,1,0:T(2,128)} %table_hbm.1, bf16[24,32,3072]{2,1,0:T(8,128)(2,1)} %bitcast.2, s32[3,1024]{1,0:T(4,128)} %class_hbm.1, s32[1,1024]{1,0:T(1,128)} %bitcast.3), custom_call_target="tpu_custom_call" | custom-call | flops 603979776 | bytes 4718592 | tf_op jit(solution)/shard_map/panel/pallas_call | solution.py:474
  62.4 1.5 %convert_reduce_fusion = f32[24,128]{1,0:T(8,128)} fusion(bf16[16,24,128]{2,1,0:T(8,128)(2,1)} %panel.1), kind=kLoop, calls=%fused_computation | loop fusion | flops 95232 | bytes 110592 | tf_op jit(solution)/shard_map/reduce_sum | solution.py:536

commit v5 on v3

--- a/solution.py
+++ b/solution.py
@@ -45,7 +45,6 @@
     coef,
     field,
     gath,
-    panel,
     product,
     sibling_in,
     part,
@@ -77,6 +76,7 @@
     groups, _, cells = sens.shape
     chips = slabs // 2
     core = lax.rem(me, 2)
+    half = cells // 2
     chip = lax.div(me, 2)
     sibling = me + 1 - 2 * core
     depth, plane = class_ref.shape
@@ -90,6 +90,13 @@
 
     def at(x_to, y_to, slab_to):
         return (x_to * 4 + y_to, slab_to)
+
+    def fold(rows):
+        return jnp.concatenate([rows[:, :half], rows[:, half:]], axis=0).astype(bf16)
+
+    def unfold(piece):
+        piece = piece.astype(f32)
+        return jnp.concatenate([piece[:PIECE], piece[PIECE:]], axis=1)
 
     def remote(src, dst, send_sem, recv_sem, target):
         return pltpu.make_async_remote_copy(
@@ -220,7 +227,8 @@
         remote(send2.at[j], recv2.at[j], s2_send.at[j], s2_recv.at[j], at(x, j, me)).wait_recv()
 
     def scatter_y(rows, first):
-        pieces = rows.astype(f32).reshape(2, PIECE, cells).astype(bf16)
+        rows = rows.astype(f32)
+        pieces = [fold(rows[:PIECE]), fold(rows[PIECE:])]
         for j in (first, first + 1):
 
             @pl.when(yh == j)
@@ -262,8 +270,9 @@
     halo_after.start()
     halo_before.start()
 
+    own_rows = unfold(raw[...])
     for g in range(depth):
-        field[0, depth + g] = raw[:, g * plane : (g + 1) * plane].astype(f32)
+        field[0, depth + g] = own_rows[:, g * plane : (g + 1) * plane]
     position = lax.broadcasted_iota(jnp.int32, (PIECE, plane), 1)
     column = lax.rem(position, WIDTH_Y)
     sweeps = table_ref.shape[0]
@@ -285,7 +294,7 @@
             field[k + 1, l] = updated
         else:
             g = l - depth
-            gath[x, 0, :, g * plane : (g + 1) * plane] = updated.astype(bf16)
+            field[0, 3 * depth + g] = updated
 
     def copy_g5(place, dj, lands):
         target = at(x, lax.rem(yh + dj, 4), me)
@@ -319,10 +328,11 @@
     halo_before.wait_recv()
     has_before = jnp.where(me > 0, 1.0, 0.0).astype(f32)
     has_after = jnp.where(me < slabs - 1, 1.0, 0.0).astype(f32)
+    rows_before = unfold(halo[0]) * has_before
+    rows_after = unfold(halo[1]) * has_after
     for g in range(depth):
-        cut = slice(g * plane, (g + 1) * plane)
-        field[0, g] = halo[0, :, cut].astype(f32) * has_before
-        field[0, 2 * depth + g] = halo[1, :, cut].astype(f32) * has_after
+        field[0, g] = rows_before[:, g * plane : (g + 1) * plane]
+        field[0, 2 * depth + g] = rows_after[:, g * plane : (g + 1) * plane]
 
     def smooth_all(k, l):
         if k < 0 or (k, l) in done:
@@ -334,12 +344,9 @@
 
     for t in range(depth):
         smooth_all(sweeps - 1, depth + t)
+    gath[x, 0] = fold(jnp.concatenate([field[0, 3 * depth + g] for g in range(depth)], axis=1))
     for copy in over_y + [to_right[0], to_left[0]]:
         copy.start()
-
-    def into_panel(source):
-        rows = gath[source].astype(f32).reshape(GROUP, cells).astype(bf16)
-        panel[pl.ds(pl.multiple_of(source * GROUP, GROUP), GROUP)] = rows
 
     wait_g5(1)
     wait_g5(2)
@@ -355,14 +362,8 @@
     from_right[0].wait_recv()
     from_right[1].wait_recv()
     relays[1].start()
-    into_panel(x)
-    from_right[2].wait_recv()
-    into_panel(right)
-    from_left[2].wait_recv()
-    into_panel(left)
-    for copy in relayed:
+    for copy in (from_left[2], from_right[2], *relayed):
         copy.wait_recv()
-    into_panel(far)
 
     data_rows = groups * GROUP
     chunk = min(CHUNK, data_rows)
@@ -383,11 +384,26 @@
 
     def multiply(turn):
         here = chunk_of(turn)
-        rows = sens[pl.ds(here * (chunk // GROUP), chunk // GROUP)].reshape(chunk, cells)
-        result = lax.dot_general(rows, panel[...], (((1,), (1,)), ((), ())), preferred_element_type=f32)
+        part_of = pl.ds(here * (chunk // GROUP), chunk // GROUP)
+        pieces = gath[...].reshape(2 * PANEL, half)
+        first, second = [
+            lax.dot_general(
+                sens[part_of, :, h * half : (h + 1) * half].reshape(chunk, half),
+                pieces,
+                (((1,), (1,)), ((), ())),
+                preferred_element_type=f32,
+            )
+            for h in range(2)
+        ]
+        lane = lax.broadcasted_iota(jnp.int32, (chunk, PANEL), 1)
+        result = jnp.where(
+            lax.rem(lane, 2 * PIECE) < PIECE,
+            first[:, :PANEL] + pltpu.roll(second[:, :PANEL], PANEL - PIECE, 1),
+            pltpu.roll(first[:, PANEL:], PIECE, 1) + second[:, PANEL:],
+        )
         result = result.reshape(blocks, 2, out_rows, PANEL)
-        for half in range(2):
-            product[turn, half] = result[:, half]
+        for c in range(2):
+            product[turn, c] = result[:, c]
         copy_sibling(turn).start()
 
     def send_parts(turn):
@@ -443,17 +459,16 @@
     for i in range(chips):
         total = total + parts_in[i].astype(f32)
     total = total * (1.0 / math.sqrt(layers * plane))
+    lane = lax.broadcasted_iota(jnp.int32, (PANEL, PANEL), 0)
+    wanted = lax.broadcasted_iota(jnp.int32, (PANEL, PANEL), 1)
+    from_x = lax.div(wanted, GROUP)
+    dj = lax.rem(lax.div(wanted, PIECE) + 4 - yh, 4)
+    place = jnp.where(dj == 2, 3, jnp.where(dj == 3, 2, dj))
+    held = 64 * lax.rem(from_x, 2) + 16 * place + 8 * lax.div(from_x, 2) + lax.rem(wanted, PIECE)
+    total = jnp.dot(
+        total, (lane == held).astype(f32), precision=lax.Precision.HIGHEST, preferred_element_type=f32
+    )
     col = lax.broadcasted_iota(jnp.int32, out_ref.shape, 1)
-    place = lax.div(lax.rem(col, GROUP), PIECE)
-    total = jnp.where(
-        place == 2, pltpu.roll(total, PANEL - PIECE, 1), jnp.where(place == 3, pltpu.roll(total, PIECE, 1), total)
-    )
-    shift = PIECE * yh
-    total = jnp.where(
-        lax.rem(col, GROUP) >= shift,
-        pltpu.roll(total, shift, 1),
-        pltpu.roll(total, shift + PANEL - GROUP, 1),
-    )
     base = dp * data_rows + me * out_rows
     row = base + lax.broadcasted_iota(jnp.int32, out_ref.shape, 0)
     out_ref[...] = jnp.where(row >= start * PANEL + col, total, 0.0)
@@ -488,16 +503,15 @@
             pltpu.VMEM((HALF, cells), bf16),
             pltpu.VMEM((2, HALF, cells), bf16),
             pltpu.VMEM((HALF, cells), bf16),
-            pltpu.VMEM((4, PIECE, cells), bf16),
-            pltpu.VMEM((4, PIECE, cells), bf16),
-            pltpu.VMEM((PIECE, cells), bf16),
-            pltpu.VMEM((2, PIECE, cells), bf16),
+            pltpu.VMEM((4, 2 * PIECE, cells // 2), bf16),
+            pltpu.VMEM((4, 2 * PIECE, cells // 2), bf16),
+            pltpu.VMEM((2 * PIECE, cells // 2), bf16),
+            pltpu.VMEM((2, 2 * PIECE, cells // 2), bf16),
             pltpu.VMEM((2, depth, plane), jnp.int32),
             pltpu.VMEM((ext, plane), jnp.int32),
             pltpu.VMEM((sweeps, 4, ext, plane), jnp.float32),
-            pltpu.VMEM((sweeps, 3 * depth, PIECE, plane), jnp.float32),
-            pltpu.VMEM((4, 4, PIECE, cells), bf16),
-            pltpu.VMEM((PANEL, cells), bf16),
+            pltpu.VMEM((sweeps, 4 * depth, PIECE, plane), jnp.float32),
+            pltpu.VMEM((4, 4, 2 * PIECE, cells // 2), bf16),
             pltpu.VMEM((chunks, 2, rows // chunks // (2 * out_rows), out_rows, PANEL), jnp.float32),
             pltpu.VMEM((chunks, rows // chunks // (2 * out_rows), out_rows, PANEL), jnp.float32),
             pltpu.VMEM((chips, out_rows, PANEL), bf16),

time: 58.6 us -> 57.7 us (0.985)
  Pallas kernels: 56.4 us -> 55.4 us
    pallas_call x1, Pallas kernels: 56.4 us -> 55.4 us  [body(): pl.pallas_call(functools.partial(kernel, slabs), out_shape=jax.ShapeDtype...]
where the time goes in v5:
time: 57.7 us; the launch traced here: 57.4 us
  Pallas kernels  55.4 us (96%)
  local copies, waits for them, and re-layouts  1.31 us (2%)
  between operations  0.66 us (1%)
    pallas_call x1, Pallas kernels, body(): pl.pallas_call(functools.partial(kernel, slabs), out_shape=jax.ShapeDtype...  55.4 us
    unnamed x1, local copies, waits for them, and re-layouts  1.31 us

profile of v5, /device:TPU:1, one launch (start us, length us, event | category | flops | bytes accessed | tf_op | source)
XLA Modules:
  0.0 57.4 jit_solution(13319771970681453403)
XLA Ops:
  0.7 55.4 %panel.1 = f32[24,128]{1,0:T(8,128)} custom-call(s32[1]{0:T(128)S(6)} %copy.7.panel_hbm, f32[3,2,8]{2,1,0:T(2,128)} %table_hbm.1, bf16[24,32,3072]{2,1,0:T(8,128)(2,1)} %bitcast.2, s32[3,1024]{1,0:T(4,128)} %class_hbm.1, s32[1,1024]{1,0:T(1,128)} %bitcast.3), custom_call_target="tpu_custom_call" | custom-call | flops 603979776 | bytes 4718592 | tf_op jit(solution)/shard_map/panel/pallas_call | solution.py:489
  56.1 1.3 %copy.8 = f32[24,128]{1,0:T(8,128)} copy(f32[24,128]{1,0:T(8,128)} %panel.1) | data formatting | bytes 24576

commit v6 on v5

--- a/solution.py
+++ b/solution.py
@@ -11,9 +11,8 @@
 WIDTH_Y = 32
 PANEL = 128
 GROUP = 32
-HALF = 16
 PIECE = 8
-CHUNK = 384
+CHUNK = 192
 VMEM_LIMIT = 63 * 1024 * 1024
 
 
@@ -120,12 +119,21 @@
             [(class_hbm, class_ref), (tear_hbm, tear_ref), (table_hbm, table_ref), (panel_hbm, panel_ref)]
         )
     ]
+    barrier = pltpu.get_barrier_semaphore()
+
+    def start_loads():
+        for i in range(loads):
+            load(i).start()
+
+    def wait_loads():
+        pltpu.make_async_copy(sens_hbm, sens, load_sem.at[0]).wait()
+
     for copy in small:
         copy.start()
-    for i in range(loads):
-        load(i).start()
-
-    barrier = pltpu.get_barrier_semaphore()
+
+    @pl.when(x < 2)
+    def _():
+        start_loads()
 
     def greet(target):
         pl.semaphore_signal(
@@ -143,9 +151,12 @@
     greet(at(left, yh, me))
     greet(at(lax.rem(x + 2, 4), yh, me))
 
+    @pl.when(x >= 2)
+    def _():
+        start_loads()
+
     for copy in small:
         copy.wait()
-    pltpu.make_async_copy(sens_hbm, sens, load_sem.at[0]).wait()
 
     start = panel_ref[0]
     owner = lax.div(start, panels_dev)
@@ -155,16 +166,19 @@
 
     @pl.when(x < 2)
     def _():
+        wait_loads()
         for q in range(4):
-            send1[q] = sens[first_group + q].reshape(2, HALF, cells)
+            rows = sens[first_group + q].astype(f32)
+            for j in range(4):
+                send1[q, lax.rem(j - yh + 6, 4)] = fold(rows[j * PIECE : (j + 1) * PIECE])
 
     pl.semaphore_wait(barrier, 8 + chips - 1)
 
     def early(q):
-        return send1.at[q, 0]
+        return send1.at[q, 0:2]
 
     def late(q):
-        return send1.at[q, 1]
+        return send1.at[q, 2:4]
 
     mate = at(1 - x, yh, me)
     outer = at(3 - x, yh, me)
@@ -183,9 +197,9 @@
     def _():
         for copy in (copy_far, copy_mate, copy_in, copy_out, copy_in_late):
             copy.start()
-        recv_early[x] = send1[x, 0]
-        recv_late[x] = send1[x, 1]
-        pair1[x] = send1[3 - x, 1]
+        recv_early[x] = send1[x, 0:2]
+        recv_late[x] = send1[x, 2:4]
+        pair1[x] = send1[3 - x, 2:4]
 
     class_after = remote(class_ref, class_halo.at[0], class_send.at[0], class_recv.at[0], (dp, after))
     class_before = remote(class_ref, class_halo.at[1], class_send.at[1], class_recv.at[1], (dp, before))
@@ -219,26 +233,14 @@
         coef[k, 2] = up
         coef[k, 3] = down
 
-    def copy_y(j):
-        return remote(send2.at[j], recv2.at[yh], s2_send.at[j], s2_recv.at[yh], at(x, j, me))
+    def copy_y(dj):
+        return remote(
+            send2.at[dj], recv2.at[yh], s2_send.at[dj], s2_recv.at[yh], at(x, lax.rem(yh + dj, 4), me)
+        )
 
     def wait_y(dj):
         j = lax.rem(yh + dj, 4)
-        remote(send2.at[j], recv2.at[j], s2_send.at[j], s2_recv.at[j], at(x, j, me)).wait_recv()
-
-    def scatter_y(rows, first):
-        rows = rows.astype(f32)
-        pieces = [fold(rows[:PIECE]), fold(rows[PIECE:])]
-        for j in (first, first + 1):
-
-            @pl.when(yh == j)
-            def _(j=j):
-                recv2[yh] = pieces[j - first]
-
-            @pl.when(yh != j)
-            def _(j=j):
-                send2[j] = pieces[j - first]
-                copy_y(j).start()
+        remote(send2.at[dj], recv2.at[j], s2_send.at[dj], s2_recv.at[j], at(x, j, me)).wait_recv()
 
     @pl.when(x >= 2)
     def _():
@@ -247,7 +249,11 @@
         arrived(3, recv_early.at[3 - x])
 
     arrived(1, recv_early.at[jnp.where(x < 2, 1 - x, x - 2)])
-    scatter_y(recv_early[x_owner], 0)
+    chosen = recv_early[x_owner]
+    send2[2] = chosen[0]
+    copy_y(2).start()
+    send2[3] = chosen[1]
+    copy_y(3).start()
 
     @pl.when(x < 2)
     def _():
@@ -260,7 +266,10 @@
     def _():
         arrived(5, recv_late.at[0])
 
-    scatter_y(recv_late[jnp.where(x < 2, x_owner, 0)], 2)
+    chosen = recv_late[jnp.where(x < 2, x_owner, 0)]
+    send2[1] = chosen[1]
+    copy_y(1).start()
+    recv2[yh] = chosen[0]
     for dj in (2, 1, 3):
         wait_y(dj)
 
@@ -364,6 +373,10 @@
     relays[1].start()
     for copy in (from_left[2], from_right[2], *relayed):
         copy.wait_recv()
+
+    @pl.when(x >= 2)
+    def _():
+        wait_loads()
 
     data_rows = groups * GROUP
     chunk = min(CHUNK, data_rows)
@@ -438,12 +451,8 @@
     def _():
         copy_on.wait_send()
 
-    for j in range(4):
-
-        @pl.when(yh != j)
-        def _(j=j):
-            copy_y(j).wait_send()
-
+    for dj in (1, 2, 3):
+        copy_y(dj).wait_send()
     for copy in over_y + to_right + to_left + relays + [to_far]:
         copy.wait_send()
     for turn in range(chunks):
@@ -497,12 +506,12 @@
             pltpu.VMEM((depth, plane), jnp.int32),
             pltpu.VMEM((1, plane), jnp.int32),
             pltpu.VMEM((groups, GROUP, cells), bf16),
-            pltpu.VMEM((4, 2, HALF, cells), bf16),
-            pltpu.VMEM((2, HALF, cells), bf16),
-            pltpu.VMEM((2, HALF, cells), bf16),
-            pltpu.VMEM((HALF, cells), bf16),
-            pltpu.VMEM((2, HALF, cells), bf16),
-            pltpu.VMEM((HALF, cells), bf16),
+            pltpu.VMEM((4, 4, 2 * PIECE, cells // 2), bf16),
+            pltpu.VMEM((2, 2, 2 * PIECE, cells // 2), bf16),
+            pltpu.VMEM((2, 2, 2 * PIECE, cells // 2), bf16),
+            pltpu.VMEM((2, 2 * PIECE, cells // 2), bf16),
+            pltpu.VMEM((2, 2, 2 * PIECE, cells // 2), bf16),
+            pltpu.VMEM((2, 2 * PIECE, cells // 2), bf16),
             pltpu.VMEM((4, 2 * PIECE, cells // 2), bf16),
             pltpu.VMEM((4, 2 * PIECE, cells // 2), bf16),
             pltpu.VMEM((2 * PIECE, cells // 2), bf16),

time: 57.7 us -> 58.3 us (1.010)
  Pallas kernels: 55.4 us -> 56 us
where the time goes in v6:
time: 58.3 us; the launch traced here: 58 us
  Pallas kernels  56 us (96%)
  local copies, waits for them, and re-layouts  1.31 us (2%)
  between operations  0.66 us (1%)
    pallas_call x1, Pallas kernels, body(): pl.pallas_call(functools.partial(kernel, slabs), out_shape=jax.ShapeDtype...  56 us
    unnamed x1, local copies, waits for them, and re-layouts  1.31 us

profile of v6, /device:TPU:1, one launch (start us, length us, event | category | flops | bytes accessed | tf_op | source)
XLA Modules:
  0.0 58.0 jit_solution(13637080288556715258)
XLA Ops:
  0.7 56.0 %panel.1 = f32[24,128]{1,0:T(8,128)} custom-call(s32[1]{0:T(128)S(6)} %copy.7.panel_hbm, f32[3,2,8]{2,1,0:T(2,128)} %table_hbm.1, bf16[24,32,3072]{2,1,0:T(8,128)(2,1)} %bitcast.2, s32[3,1024]{1,0:T(4,128)} %class_hbm.1, s32[1,1024]{1,0:T(1,128)} %bitcast.3), custom_call_target="tpu_custom_call" | custom-call | flops 603979776 | bytes 4718592 | tf_op jit(solution)/shard_map/panel/pallas_call | solution.py:498
  56.7 1.3 %copy.8 = f32[24,128]{1,0:T(8,128)} copy(f32[24,128]{1,0:T(8,128)} %panel.1) | data formatting | bytes 24576

commit v7 on v6

--- a/solution.py
+++ b/solution.py
@@ -47,7 +47,6 @@
     product,
     sibling_in,
     part,
-    parts_in,
     load_sem,
     class_send,
     class_recv,
@@ -80,7 +79,7 @@
     sibling = me + 1 - 2 * core
     depth, plane = class_ref.shape
     layers = depth * slabs
-    out_rows = out_ref.shape[0]
+    out_rows = out_ref.shape[1]
     panels_dev = groups * GROUP // PANEL
     right = lax.rem(x + 1, 4)
     left = lax.rem(x + 3, 4)
@@ -324,9 +323,9 @@
     to_left = [copy_g6(left, x, *span, 3 + i) for i, span in enumerate(rounds)]
     from_left = [copy_g6(right, left, *span, i) for i, span in enumerate(rounds)]
     from_right = [copy_g6(left, right, *span, 3 + i) for i, span in enumerate(rounds)]
-    relays = [copy_g6(right, left, 0, 2, 6), copy_g6(left, right, 2, 3, 7)]
-    to_far = copy_g6(far, x, 3, 4, 8)
-    relayed = [copy_g6(right, far, 0, 2, 6), copy_g6(left, far, 2, 3, 7), copy_g6(far, far, 3, 4, 8)]
+    to_far = [copy_g6(far, x, 1, 3, 6), copy_g6(far, x, 3, 4, 7)]
+    relay = copy_g6(left, right, 0, 1, 8)
+    from_far = [copy_g6(far, far, 1, 3, 6), copy_g6(far, far, 3, 4, 7), copy_g6(left, far, 0, 1, 8)]
 
     inner = [(0, l) for l in range(depth + 1, 2 * depth - 1)]
     done = set(inner)
@@ -359,19 +358,16 @@
 
     wait_g5(1)
     wait_g5(2)
+    to_far[0].start()
     to_right[1].start()
     to_left[1].start()
+    from_right[0].wait_recv()
+    relay.start()
     wait_g5(3)
-    to_far.start()
+    to_far[1].start()
     to_right[2].start()
     to_left[2].start()
-    from_left[0].wait_recv()
-    from_left[1].wait_recv()
-    relays[0].start()
-    from_right[0].wait_recv()
-    from_right[1].wait_recv()
-    relays[1].start()
-    for copy in (from_left[2], from_right[2], *relayed):
+    for copy in (from_left[0], *from_left[1:], *from_right[1:], *from_far):
         copy.wait_recv()
 
     @pl.when(x >= 2)
@@ -390,7 +386,7 @@
         )
 
     def copy_part(to):
-        return remote(part.at[to], parts_in.at[chip], rs_send.at[0], rs_recv.at[0], (dp, 2 * to + core))
+        return remote(part.at[to], out_ref.at[chip], rs_send.at[0], rs_recv.at[0], (dp, 2 * to + core))
 
     def chunk_of(turn):
         return lax.rem(own_chunk + 1 + turn, chunks)
@@ -422,7 +418,23 @@
     def send_parts(turn):
         here = chunk_of(turn)
         copy_sibling(turn).wait_recv()
-        part[pl.ds(here * blocks, blocks)] = (product[turn, core] + sibling_in[turn]).astype(bf16)
+        total = (product[turn, core] + sibling_in[turn]) * (1.0 / math.sqrt(layers * plane))
+        lane = lax.broadcasted_iota(jnp.int32, (PANEL, PANEL), 0)
+        wanted = lax.broadcasted_iota(jnp.int32, (PANEL, PANEL), 1)
+        from_x = lax.div(wanted, GROUP)
+        dj = lax.rem(lax.div(wanted, PIECE) + 4 - yh, 4)
+        place = jnp.where(dj == 2, 3, jnp.where(dj == 3, 2, dj))
+        held = 64 * lax.rem(from_x, 2) + 16 * place + 8 * lax.div(from_x, 2) + lax.rem(wanted, PIECE)
+        total = jnp.dot(
+            total.reshape(blocks * out_rows, PANEL),
+            (lane == held).astype(f32),
+            precision=lax.Precision.HIGHEST,
+            preferred_element_type=f32,
+        ).reshape(blocks, out_rows, PANEL)
+        block = here * blocks + lax.broadcasted_iota(jnp.int32, total.shape, 0)
+        row = dp * data_rows + (2 * block + core) * out_rows + lax.broadcasted_iota(jnp.int32, total.shape, 1)
+        col = lax.broadcasted_iota(jnp.int32, total.shape, 2)
+        part[pl.ds(here * blocks, blocks)] = jnp.where(row >= start * PANEL + col, total, 0.0).astype(bf16)
         for i in range(blocks):
             to = here * blocks + i
 
@@ -435,7 +447,8 @@
         if turn > 0:
             send_parts(turn - 1)
     send_parts(chunks - 1)
-    parts_in[chip] = part[chip]
+    own_part = pltpu.make_async_copy(part.at[chip], out_ref.at[chip], rs_send.at[1])
+    own_part.start()
 
     class_after.wait_send()
     class_before.wait_send()
@@ -453,34 +466,17 @@
 
     for dj in (1, 2, 3):
         copy_y(dj).wait_send()
-    for copy in over_y + to_right + to_left + relays + [to_far]:
+    for copy in over_y + to_right + to_left + to_far + [relay]:
         copy.wait_send()
     for turn in range(chunks):
         copy_sibling(turn).wait_send()
 
     others = remote(
-        part.at[0 : chips - 1], parts_in.at[0 : chips - 1], rs_send.at[0], rs_recv.at[0], (dp, sibling)
+        part.at[0 : chips - 1], out_ref.at[0 : chips - 1], rs_send.at[0], rs_recv.at[0], (dp, sibling)
     )
     others.wait_send()
     others.wait_recv()
-
-    total = jnp.zeros(out_ref.shape, f32)
-    for i in range(chips):
-        total = total + parts_in[i].astype(f32)
-    total = total * (1.0 / math.sqrt(layers * plane))
-    lane = lax.broadcasted_iota(jnp.int32, (PANEL, PANEL), 0)
-    wanted = lax.broadcasted_iota(jnp.int32, (PANEL, PANEL), 1)
-    from_x = lax.div(wanted, GROUP)
-    dj = lax.rem(lax.div(wanted, PIECE) + 4 - yh, 4)
-    place = jnp.where(dj == 2, 3, jnp.where(dj == 3, 2, dj))
-    held = 64 * lax.rem(from_x, 2) + 16 * place + 8 * lax.div(from_x, 2) + lax.rem(wanted, PIECE)
-    total = jnp.dot(
-        total, (lane == held).astype(f32), precision=lax.Precision.HIGHEST, preferred_element_type=f32
-    )
-    col = lax.broadcasted_iota(jnp.int32, out_ref.shape, 1)
-    base = dp * data_rows + me * out_rows
-    row = base + lax.broadcasted_iota(jnp.int32, out_ref.shape, 0)
-    out_ref[...] = jnp.where(row >= start * PANEL + col, total, 0.0)
+    own_part.wait()
 
 
 def body(sensitivity, panel_index, cell_class, tear_layer, coef_table):
@@ -495,11 +491,11 @@
     dma = pltpu.SemaphoreType.DMA
     sweeps = coef_table.shape[0]
     ext = -(-(depth + 4) // 8) * 8
-    return pl.pallas_call(
+    parts = pl.pallas_call(
         functools.partial(kernel, slabs),
-        out_shape=jax.ShapeDtypeStruct((out_rows, PANEL), jnp.float32),
+        out_shape=jax.ShapeDtypeStruct((chips, out_rows, PANEL), bf16),
         in_specs=[pl.BlockSpec(memory_space=pltpu.HBM)] * 5,
-        out_specs=pl.BlockSpec(memory_space=pltpu.VMEM),
+        out_specs=pl.BlockSpec(memory_space=pltpu.HBM),
         scratch_shapes=[
             pltpu.SMEM(panel_index.shape, jnp.int32),
             pltpu.SMEM(coef_table.shape, jnp.float32),
@@ -524,7 +520,6 @@
             pltpu.VMEM((chunks, 2, rows // chunks // (2 * out_rows), out_rows, PANEL), jnp.float32),
             pltpu.VMEM((chunks, rows // chunks // (2 * out_rows), out_rows, PANEL), jnp.float32),
             pltpu.VMEM((chips, out_rows, PANEL), bf16),
-            pltpu.VMEM((chips, out_rows, PANEL), bf16),
             dma((5,)),
             dma((2,)),
             dma((2,)),
@@ -540,7 +535,7 @@
             dma((9,)),
             dma((chunks,)),
             dma((chunks,)),
-            dma((1,)),
+            dma((2,)),
             dma((1,)),
         ],
         compiler_params=pltpu.CompilerParams(
@@ -557,6 +552,7 @@
         cell_class,
         tear_layer.reshape(1, plane),
     )
+    return parts.astype(jnp.float32).sum(axis=0)
 
 
 def solution(mesh):

time: 58.3 us -> 57.8 us (level)
  other arithmetic: 0 us -> 1.51 us
  local copies, waits for them, and re-layouts: 1.31 us -> 0 us
  Pallas kernels: 56 us -> 55.4 us
    reduce_sum x0 -> x1, other arithmetic: none -> 1.51 us  [body(): return parts.astype(jnp.float32).sum(axis=0)]
    unnamed x1 -> x0, local copies, waits for them, and re-layouts: 1.31 us -> none
    pallas_call x1, Pallas kernels: 56 us -> 55.4 us  [body(): pl.pallas_call(functools.partial(kernel, slabs), out_shape=jax.ShapeDtype...]
where the time goes in v7:
time: 57.8 us; the launch traced here: 57.6 us
  Pallas kernels  55.4 us (96%)
  other arithmetic  1.51 us (3%)
  between operations  0.66 us (1%)
    pallas_call x1, Pallas kernels, body(): pl.pallas_call(functools.partial(kernel, slabs), out_shape=jax.ShapeDtype...  55.4 us
    reduce_sum x1, other arithmetic, body(): return parts.astype(jnp.float32).sum(axis=0)  1.51 us

profile of v7, /device:TPU:1, one launch (start us, length us, event | category | flops | bytes accessed | tf_op | source)
XLA Modules:
  0.0 57.6 jit_solution(12251600964123929694)
XLA Ops:
  0.7 55.4 %panel.1 = bf16[16,24,128]{2,1,0:T(8,128)(2,1)} custom-call(s32[1]{0:T(128)S(6)} %copy.6.panel_hbm, f32[3,2,8]{2,1,0:T(2,128)} %table_hbm.1, bf16[24,32,3072]{2,1,0:T(8,128)(2,1)} %bitcast.2, s32[3,1024]{1,0:T(4,128)} %class_hbm.1, s32[1,1024]{1,0:T(1,128)} %bitcast.3), custom_call_target="tpu_custom_call" | custom-call | flops 603979776 | bytes 4718592 | tf_op jit(solution)/shard_map/panel/pallas_call | solution.py:494
  56.1 1.5 %convert_reduce_fusion = f32[24,128]{1,0:T(8,128)} fusion(bf16[16,24,128]{2,1,0:T(8,128)(2,1)} %panel.1), kind=kLoop, calls=%fused_computation | loop fusion | flops 95232 | bytes 110592 | tf_op jit(solution)/shard_map/reduce_sum | solution.py:555

commit v8 on v7

--- a/solution.py
+++ b/solution.py
@@ -139,7 +139,8 @@
             barrier, inc=1, device_id=target, device_id_type=pl.DeviceIdType.MESH
         )
 
-    for d in sorted(range(1, chips), key=lambda d: -min(d, chips - d)):
+    @pl.loop(1, chips)
+    def _(d):
         greet((dp, lax.rem(me + 2 * d, slabs)))
 
     for dj in (2, 1, 3):
@@ -166,7 +167,9 @@
     @pl.when(x < 2)
     def _():
         wait_loads()
-        for q in range(4):
+
+        @pl.loop(0, 4)
+        def _(q):
             rows = sens[first_group + q].astype(f32)
             for j in range(4):
                 send1[q, lax.rem(j - yh + 6, 4)] = fold(rows[j * PIECE : (j + 1) * PIECE])
@@ -217,7 +220,8 @@
     tear = jnp.broadcast_to(tear_ref[...], classes.shape)
     open_up = tear != layer
     open_down = tear != layer + 1
-    for k in range(table_ref.shape[0]):
+    @pl.loop(0, table_ref.shape[0])
+    def _(k):
         a = jnp.zeros(classes.shape, f32)
         b = jnp.zeros(classes.shape, f32)
         for level in range(table_ref.shape[2]):
@@ -291,12 +295,12 @@
         south = jnp.where(position < plane - WIDTH_Y, pltpu.roll(u, plane - WIDTH_Y, 1), 0.0)
         west = jnp.where(column > 0, pltpu.roll(u, 1, 1), 0.0)
         east = jnp.where(column < WIDTH_Y - 1, pltpu.roll(u, plane - 1, 1), 0.0)
-        e = l - depth + 2
+        row = pl.ds(l - depth + 2, 1)
         updated = (
-            coef[k, 0, e : e + 1] * u
-            + coef[k, 1, e : e + 1] * ((north + south) + (west + east))
-            + coef[k, 2, e : e + 1] * field[k, l - 1]
-            + coef[k, 3, e : e + 1] * field[k, l + 1]
+            coef[k, 0, row] * u
+            + coef[k, 1, row] * ((north + south) + (west + east))
+            + coef[k, 2, row] * field[k, l - 1]
+            + coef[k, 3, row] * field[k, l + 1]
         )
         if k + 1 < sweeps:
             field[k + 1, l] = updated
@@ -327,11 +331,6 @@
     relay = copy_g6(left, right, 0, 1, 8)
     from_far = [copy_g6(far, far, 1, 3, 6), copy_g6(far, far, 3, 4, 7), copy_g6(left, far, 0, 1, 8)]
 
-    inner = [(0, l) for l in range(depth + 1, 2 * depth - 1)]
-    done = set(inner)
-    for k, l in inner:
-        smooth(k, l)
-
     halo_after.wait_recv()
     halo_before.wait_recv()
     has_before = jnp.where(me > 0, 1.0, 0.0).astype(f32)
@@ -342,16 +341,12 @@
         field[0, g] = rows_before[:, g * plane : (g + 1) * plane]
         field[0, 2 * depth + g] = rows_after[:, g * plane : (g + 1) * plane]
 
-    def smooth_all(k, l):
-        if k < 0 or (k, l) in done:
-            return
-        for near in (l - 1, l, l + 1):
-            smooth_all(k - 1, near)
-        smooth(k, l)
-        done.add((k, l))
-
-    for t in range(depth):
-        smooth_all(sweeps - 1, depth + t)
+    for k in range(sweeps):
+
+        @pl.loop(k + 1, 3 * depth - k - 1)
+        def _(l, k=k):
+            smooth(k, l)
+
     gath[x, 0] = fold(jnp.concatenate([field[0, 3 * depth + g] for g in range(depth)], axis=1))
     for copy in over_y + [to_right[0], to_left[0]]:
         copy.start()
@@ -435,18 +430,25 @@
         row = dp * data_rows + (2 * block + core) * out_rows + lax.broadcasted_iota(jnp.int32, total.shape, 1)
         col = lax.broadcasted_iota(jnp.int32, total.shape, 2)
         part[pl.ds(here * blocks, blocks)] = jnp.where(row >= start * PANEL + col, total, 0.0).astype(bf16)
-        for i in range(blocks):
+
+        @pl.loop(0, blocks)
+        def _(i):
             to = here * blocks + i
 
             @pl.when(to != chip)
-            def _(to=to):
+            def _():
                 copy_part(to).start()
 
-    for turn in range(chunks):
-        multiply(turn)
-        if turn > 0:
+    @pl.loop(0, chunks + 1)
+    def _(turn):
+        @pl.when(turn < chunks)
+        def _():
+            multiply(turn)
+
+        @pl.when(turn > 0)
+        def _():
             send_parts(turn - 1)
-    send_parts(chunks - 1)
+
     own_part = pltpu.make_async_copy(part.at[chip], out_ref.at[chip], rs_send.at[1])
     own_part.start()
 

time: 57.8 us -> 59 us (1.021)
  Pallas kernels: 55.4 us -> 56.6 us
    pallas_call x1, Pallas kernels: 55.4 us -> 56.6 us  [body(): pl.pallas_call(functools.partial(kernel, slabs), out_shape=jax.ShapeDtype...]
where the time goes in v8:
time: 59 us; the launch traced here: 58.8 us
  Pallas kernels  56.6 us (96%)
  other arithmetic  1.51 us (3%)
  between operations  0.66 us (1%)
    pallas_call x1, Pallas kernels, body(): pl.pallas_call(functools.partial(kernel, slabs), out_shape=jax.ShapeDtype...  56.6 us
    reduce_sum x1, other arithmetic, body(): return parts.astype(jnp.float32).sum(axis=0)  1.51 us

profile of v8, /device:TPU:1, one launch (start us, length us, event | category | flops | bytes accessed | tf_op | source)
XLA Modules:
  0.0 58.8 jit_solution(17586555480199652965)
XLA Ops:
  0.7 56.6 %panel.1 = bf16[16,24,128]{2,1,0:T(8,128)(2,1)} custom-call(s32[1]{0:T(128)S(6)} %copy.6.panel_hbm, f32[3,2,8]{2,1,0:T(2,128)} %table_hbm.1, bf16[24,32,3072]{2,1,0:T(8,128)(2,1)} %bitcast.2, s32[3,1024]{1,0:T(4,128)} %class_hbm.1, s32[1,1024]{1,0:T(1,128)} %bitcast.3), custom_call_target="tpu_custom_call" | custom-call | flops 603979776 | bytes 4718592 | tf_op jit(solution)/shard_map/panel/pallas_call | solution.py:496
  57.3 1.5 %convert_reduce_fusion = f32[24,128]{1,0:T(8,128)} fusion(bf16[16,24,128]{2,1,0:T(8,128)(2,1)} %panel.1), kind=kLoop, calls=%fused_computation | loop fusion | flops 95232 | bytes 110592 | tf_op jit(solution)/shard_map/reduce_sum | solution.py:557

commit v9 on v7

--- a/solution.py
+++ b/solution.py
@@ -308,7 +308,7 @@
         target = at(x, lax.rem(yh + dj, 4), me)
         return remote(gath.at[x, 0], gath.at[x, lands], g5_send.at[place], g5_recv.at[lands], target)
 
-    over_y = [copy_g5(3, 2, 3), copy_g5(1, 1, 2), copy_g5(2, 3, 1)]
+    over_y = [copy_g5(1, 1, 2), copy_g5(2, 3, 1), copy_g5(3, 2, 3)]
 
     def wait_g5(place):
         remote(gath.at[x, 0], gath.at[x, place], g5_send.at[place], g5_recv.at[place], at(right, yh, me)).wait_recv()
@@ -323,9 +323,9 @@
     to_left = [copy_g6(left, x, *span, 3 + i) for i, span in enumerate(rounds)]
     from_left = [copy_g6(right, left, *span, i) for i, span in enumerate(rounds)]
     from_right = [copy_g6(left, right, *span, 3 + i) for i, span in enumerate(rounds)]
-    to_far = [copy_g6(far, x, 1, 3, 6), copy_g6(far, x, 3, 4, 7)]
-    relay = copy_g6(left, right, 0, 1, 8)
-    from_far = [copy_g6(far, far, 1, 3, 6), copy_g6(far, far, 3, 4, 7), copy_g6(left, far, 0, 1, 8)]
+    relays = [copy_g6(right, left, 0, 2, 6), copy_g6(left, right, 2, 3, 7)]
+    to_far = copy_g6(far, x, 3, 4, 8)
+    relayed = [copy_g6(right, far, 0, 2, 6), copy_g6(left, far, 2, 3, 7), copy_g6(far, far, 3, 4, 8)]
 
     inner = [(0, l) for l in range(depth + 1, 2 * depth - 1)]
     done = set(inner)
@@ -353,21 +353,24 @@
     for t in range(depth):
         smooth_all(sweeps - 1, depth + t)
     gath[x, 0] = fold(jnp.concatenate([field[0, 3 * depth + g] for g in range(depth)], axis=1))
-    for copy in over_y + [to_right[0], to_left[0]]:
+    for copy in [*over_y[:2], to_right[0], to_left[0], over_y[2]]:
         copy.start()
 
     wait_g5(1)
     wait_g5(2)
-    to_far[0].start()
     to_right[1].start()
     to_left[1].start()
-    from_right[0].wait_recv()
-    relay.start()
     wait_g5(3)
-    to_far[1].start()
+    to_far.start()
     to_right[2].start()
     to_left[2].start()
-    for copy in (from_left[0], *from_left[1:], *from_right[1:], *from_far):
+    from_left[0].wait_recv()
+    from_left[1].wait_recv()
+    relays[0].start()
+    from_right[0].wait_recv()
+    from_right[1].wait_recv()
+    relays[1].start()
+    for copy in (from_left[2], from_right[2], *relayed):
         copy.wait_recv()
 
     @pl.when(x >= 2)
@@ -466,7 +469,7 @@
 
     for dj in (1, 2, 3):
         copy_y(dj).wait_send()
-    for copy in over_y + to_right + to_left + to_far + [relay]:
+    for copy in over_y + to_right + to_left + relays + [to_far]:
         copy.wait_send()
     for turn in range(chunks):
         copy_sibling(turn).wait_send()

time: 57.8 us -> 56.3 us (0.974)
  Pallas kernels: 55.4 us -> 53.9 us
    pallas_call x1, Pallas kernels: 55.4 us -> 53.9 us  [body(): pl.pallas_call(functools.partial(kernel, slabs), out_shape=jax.ShapeDtype...]
where the time goes in v9:
time: 56.3 us; the launch traced here: 56.1 us
  Pallas kernels  53.9 us (96%)
  other arithmetic  1.51 us (3%)
  between operations  0.66 us (1%)
    pallas_call x1, Pallas kernels, body(): pl.pallas_call(functools.partial(kernel, slabs), out_shape=jax.ShapeDtype...  53.9 us
    reduce_sum x1, other arithmetic, body(): return parts.astype(jnp.float32).sum(axis=0)  1.51 us

profile of v9, /device:TPU:1, one launch (start us, length us, event | category | flops | bytes accessed | tf_op | source)
XLA Modules:
  0.0 56.1 jit_solution(17208716536406507442)
XLA Ops:
  0.7 53.9 %panel.1 = bf16[16,24,128]{2,1,0:T(8,128)(2,1)} custom-call(s32[1]{0:T(128)S(6)} %copy.6.panel_hbm, f32[3,2,8]{2,1,0:T(2,128)} %table_hbm.1, bf16[24,32,3072]{2,1,0:T(8,128)(2,1)} %bitcast.2, s32[3,1024]{1,0:T(4,128)} %class_hbm.1, s32[1,1024]{1,0:T(1,128)} %bitcast.3), custom_call_target="tpu_custom_call" | custom-call | flops 603979776 | bytes 4718592 | tf_op jit(solution)/shard_map/panel/pallas_call | solution.py:497
  54.6 1.5 %convert_reduce_fusion = f32[24,128]{1,0:T(8,128)} fusion(bf16[16,24,128]{2,1,0:T(8,128)(2,1)} %panel.1), kind=kLoop, calls=%fused_computation | loop fusion | flops 95232 | bytes 110592 | tf_op jit(solution)/shard_map/reduce_sum | solution.py:558

commit v10 on v9

--- a/solution.py
+++ b/solution.py
@@ -323,9 +323,14 @@
     to_left = [copy_g6(left, x, *span, 3 + i) for i, span in enumerate(rounds)]
     from_left = [copy_g6(right, left, *span, i) for i, span in enumerate(rounds)]
     from_right = [copy_g6(left, right, *span, 3 + i) for i, span in enumerate(rounds)]
-    relays = [copy_g6(right, left, 0, 2, 6), copy_g6(left, right, 2, 3, 7)]
+    relays = [copy_g6(right, left, 0, 1, 6), copy_g6(right, left, 1, 2, 9), copy_g6(left, right, 2, 3, 7)]
     to_far = copy_g6(far, x, 3, 4, 8)
-    relayed = [copy_g6(right, far, 0, 2, 6), copy_g6(left, far, 2, 3, 7), copy_g6(far, far, 3, 4, 8)]
+    relayed = [
+        copy_g6(right, far, 0, 1, 6),
+        copy_g6(right, far, 1, 2, 9),
+        copy_g6(left, far, 2, 3, 7),
+        copy_g6(far, far, 3, 4, 8),
+    ]
 
     inner = [(0, l) for l in range(depth + 1, 2 * depth - 1)]
     done = set(inner)
@@ -356,6 +361,8 @@
     for copy in [*over_y[:2], to_right[0], to_left[0], over_y[2]]:
         copy.start()
 
+    from_left[0].wait_recv()
+    relays[0].start()
     wait_g5(1)
     wait_g5(2)
     to_right[1].start()
@@ -364,12 +371,11 @@
     to_far.start()
     to_right[2].start()
     to_left[2].start()
-    from_left[0].wait_recv()
     from_left[1].wait_recv()
-    relays[0].start()
+    relays[1].start()
     from_right[0].wait_recv()
     from_right[1].wait_recv()
-    relays[1].start()
+    relays[2].start()
     for copy in (from_left[2], from_right[2], *relayed):
         copy.wait_recv()
 
@@ -534,8 +540,8 @@
             dma((2,)),
             dma((4,)),
             dma((4,)),
-            dma((9,)),
-            dma((9,)),
+            dma((10,)),
+            dma((10,)),
             dma((chunks,)),
             dma((chunks,)),
             dma((2,)),

time: 56.3 us -> 56 us (level)
  no operation moved by 1% of the time
where the time goes in v10:
time: 56 us; the launch traced here: 55.8 us
  Pallas kernels  53.6 us (96%)
  other arithmetic  1.51 us (3%)
  between operations  0.66 us (1%)
    pallas_call x1, Pallas kernels, body(): pl.pallas_call(functools.partial(kernel, slabs), out_shape=jax.ShapeDtype...  53.6 us
    reduce_sum x1, other arithmetic, body(): return parts.astype(jnp.float32).sum(axis=0)  1.51 us

profile of v10, /device:TPU:1, one launch (start us, length us, event | category | flops | bytes accessed | tf_op | source)
XLA Modules:
  0.0 55.8 jit_solution(16543891409482360741)
XLA Ops:
  0.7 53.6 %panel.1 = bf16[16,24,128]{2,1,0:T(8,128)(2,1)} custom-call(s32[1]{0:T(128)S(6)} %copy.6.panel_hbm, f32[3,2,8]{2,1,0:T(2,128)} %table_hbm.1, bf16[24,32,3072]{2,1,0:T(8,128)(2,1)} %bitcast.2, s32[3,1024]{1,0:T(4,128)} %class_hbm.1, s32[1,1024]{1,0:T(1,128)} %bitcast.3), custom_call_target="tpu_custom_call" | custom-call | flops 603979776 | bytes 4718592 | tf_op jit(solution)/shard_map/panel/pallas_call | solution.py:503
  54.3 1.5 %convert_reduce_fusion = f32[24,128]{1,0:T(8,128)} fusion(bf16[16,24,128]{2,1,0:T(8,128)(2,1)} %panel.1), kind=kLoop, calls=%fused_computation | loop fusion | flops 95232 | bytes 110592 | tf_op jit(solution)/shard_map/reduce_sum | solution.py:564

commit v11 on v10

--- a/solution.py
+++ b/solution.py
@@ -358,7 +358,7 @@
     for t in range(depth):
         smooth_all(sweeps - 1, depth + t)
     gath[x, 0] = fold(jnp.concatenate([field[0, 3 * depth + g] for g in range(depth)], axis=1))
-    for copy in [*over_y[:2], to_right[0], to_left[0], over_y[2]]:
+    for copy in [*over_y, to_right[0], to_left[0]]:
         copy.start()
 
     from_left[0].wait_recv()

time: 56 us -> 56 us (level)
  no operation moved by 1% of the time
where the time goes in v11:
time: 56 us; the launch traced here: 55.8 us
  Pallas kernels  53.6 us (96%)
  other arithmetic  1.51 us (3%)
  between operations  0.66 us (1%)
    pallas_call x1, Pallas kernels, body(): pl.pallas_call(functools.partial(kernel, slabs), out_shape=jax.ShapeDtype...  53.6 us
    reduce_sum x1, other arithmetic, body(): return parts.astype(jnp.float32).sum(axis=0)  1.51 us

profile of v11, /device:TPU:1, one launch (start us, length us, event | category | flops | bytes accessed | tf_op | source)
XLA Modules:
  0.0 55.8 jit_solution(5611258419732456462)
XLA Ops:
  0.7 53.6 %panel.1 = bf16[16,24,128]{2,1,0:T(8,128)(2,1)} custom-call(s32[1]{0:T(128)S(6)} %copy.6.panel_hbm, f32[3,2,8]{2,1,0:T(2,128)} %table_hbm.1, bf16[24,32,3072]{2,1,0:T(8,128)(2,1)} %bitcast.2, s32[3,1024]{1,0:T(4,128)} %class_hbm.1, s32[1,1024]{1,0:T(1,128)} %bitcast.3), custom_call_target="tpu_custom_call" | custom-call | flops 603979776 | bytes 4718592 | tf_op jit(solution)/shard_map/panel/pallas_call | solution.py:503
  54.3 1.5 %convert_reduce_fusion = f32[24,128]{1,0:T(8,128)} fusion(bf16[16,24,128]{2,1,0:T(8,128)(2,1)} %panel.1), kind=kLoop, calls=%fused_computation | loop fusion | flops 95232 | bytes 110592 | tf_op jit(solution)/shard_map/reduce_sum | solution.py:564
